TPU v7x, 512 devices: a whole 4x8x8 slice. The times are simulated.
512 devices in a mesh: grp: 64 (over z, y_lo, core), mdl: 8 (over y_hi, x).
Axes of the slice: x: 4, y: 8 (y_hi: 2, y_lo: 4; y = y_hi * 4 + y_lo), z: 8, core: 2. Of those that a mesh axis runs over, the one named last changes fastest.
Arguments:
- model: float32 [4096, 8, 128], P(None, 'mdl'), may hold values from -1 to 1.5
- source: float32 [1024, 3, 8, 4096], P(('grp', 'mdl')), may hold values from -6 to 6
- observed: float32 [1024, 3, 8, 4096], P(('grp', 'mdl')), may hold values from -6 to 6
- owner_ids: int32 [1024, 8, 1], P(('grp', 'mdl')), may hold values from 0 to 7; in each aligned block of 16 rows (0 to 15, 16 to 31, ..., all dimensions but the last counted through in order) at most 4 rows name the same one
- offsets: int32 [1024, 8], P(('grp', 'mdl')), may hold values from 0 to 4064
- lengths: int32 [1024, 8], P(('grp', 'mdl')), may hold values from 1 to 32, 192 in all within a row
Outputs:
- gradient: float32 [4096, 8, 128], P('grp', 'mdl')
Inputs may be any that keep to these rules, and one draw needn't show every extreme that they name: `owner_ids`: among the layers of the soundings of one device (aligned blocks of 16 layers), no owner is named by more than 4 layers; in some blocks one owner is named by exactly 4. A layer covers rows offsets to offsets + lengths - 1 of its owner's block. The first lengths rows of a layer lie in the earth, the others in the air; a sounding's 8 lengths sum to 192.
All inputs are finite; a program needn't handle non-finite values.
Results may differ from a plain program's by a relative error of at most 0.0003.
Values sent between devices are 32-bit elements; how exact they have to be, the bound alone decides.
A program may use at most 64 MiB of HBM per device.

v0:
```python
import jax
import jax.numpy as jnp
from jax import lax
from jax.sharding import PartitionSpec as P

LY = 64
LZ = 8
STEPS_FWD = 4
STEPS_ADJ = 4
LAYER = 4096
TILE = 32


AIR = 0.05
OMEGA = 0.5
BETA = 0.5


def shift_next(field, count):
    filler = jnp.zeros(field.shape[:-1] + (count,), field.dtype)
    return jnp.concatenate([field[..., count:], filler], axis=-1)


def shift_prev(field, count):
    filler = jnp.zeros(field.shape[:-1] + (count,), field.dtype)
    return jnp.concatenate([filler, field[..., :-count]], axis=-1)


def layer_masks(width):
    column = jnp.arange(LAYER, dtype=jnp.int32) % width
    return ((column != width - 1).astype(jnp.float32), (column != 0).astype(jnp.float32))


def forward_diff(field, which, masks):
    if which == 0:
        return shift_next(field, LY) - field
    if which == 1:
        return shift_next(field, 1) * masks[0] - field
    deeper = jnp.concatenate([field[:, 1:], jnp.zeros_like(field[:, :1])], axis=1)
    return deeper - field


def adjoint_diff(field, which, masks):
    if which == 0:
        return shift_prev(field, LY) - field
    if which == 1:
        return shift_prev(field, 1) * masks[1] - field
    upper = jnp.concatenate([jnp.zeros_like(field[:, :1]), field[:, :-1]], axis=1)
    return upper - field


def apply_operator(field, conduct, masks):
    east, north, vertical = (field[:, 0], field[:, 1], field[:, 2])
    curl_x = forward_diff(vertical, 1, masks) - forward_diff(north, 2, masks)
    curl_y = forward_diff(east, 2, masks) - forward_diff(vertical, 0, masks)
    curl_z = forward_diff(north, 0, masks) - forward_diff(east, 1, masks)
    back_x = adjoint_diff(curl_y, 2, masks) - adjoint_diff(curl_z, 1, masks)
    back_y = adjoint_diff(curl_z, 0, masks) - adjoint_diff(curl_x, 2, masks)
    back_z = adjoint_diff(curl_x, 1, masks) - adjoint_diff(curl_y, 0, masks)
    return jnp.stack([back_x, back_y, back_z], axis=1) + conduct[:, None] * field


def relax(right_side, conduct, count, masks):
    state = jnp.zeros_like(right_side)
    scale = OMEGA / (4.0 + conduct[:, None])
    for sweep in range(count):
        state = state + scale * (right_side - apply_operator(state, conduct, masks))
    return state


def sounding_partial(source, observed, conduct, earth, masks):
    efield = relax(source, conduct, STEPS_FWD, masks)
    adjoint_field = relax(efield - observed, conduct, STEPS_ADJ, masks)
    return -conduct * jnp.sum(efield * adjoint_field, axis=1) * earth


def smoothing(values):
    left = jnp.concatenate([values[..., :1], values[..., :-1]], axis=-1)
    right = jnp.concatenate([values[..., 1:], values[..., -1:]], axis=-1)
    return BETA * (2.0 * values - left - right)


def place_slots(owner_flat, owners_count, capacity):
    chosen = (owner_flat[:, None] == jnp.arange(owners_count, dtype=jnp.int32)[None, :]).astype(
        jnp.int32
    )
    before = jnp.cumsum(chosen, axis=0) - chosen
    return owner_flat * capacity + jnp.sum(before * chosen, axis=1)


def settle(block, source, observed, owner_ids, offsets, lengths, owners_count, capacity, masks):
    count = source.shape[0]
    tiles = count * LZ
    within = jnp.arange(TILE, dtype=jnp.int32)
    places = place_slots(owner_ids.reshape(tiles), owners_count, capacity)
    request = (
        jnp.zeros((owners_count * capacity,), jnp.int32).at[places].set(offsets.reshape(tiles))
    )
    request = request.reshape(owners_count, capacity)
    values = jnp.exp(
        block[
            lax.all_to_all(request, "mdl", split_axis=0, concat_axis=0, tiled=True)[..., None]
            + within
        ]
    )
    answer = lax.all_to_all(values, "mdl", split_axis=0, concat_axis=0, tiled=True)
    fetched = answer.reshape(owners_count * capacity, TILE, 128)[places].reshape(count, LZ, LAYER)
    earth = (within[None, :] < lengths.reshape(tiles)[:, None]).astype(jnp.float32)
    earth = jnp.broadcast_to(earth[..., None], (tiles, TILE, 128)).reshape(count, LZ, LAYER)
    conduct = jnp.where(earth > 0.5, fetched, AIR)
    partial_value = sounding_partial(source, observed, conduct, earth, masks)
    outgoing = jnp.zeros((owners_count * capacity, TILE, 128), jnp.float32)
    outgoing = outgoing.at[places].set(partial_value.reshape(tiles, TILE, 128))
    outgoing = outgoing.reshape(owners_count, capacity, TILE, 128)
    arrived, arrived_starts = (
        lax.all_to_all(outgoing, "mdl", split_axis=0, concat_axis=0, tiled=True),
        lax.all_to_all(request, "mdl", split_axis=0, concat_axis=0, tiled=True),
    )
    target_rows = (arrived_starts[..., None] + within).reshape(-1)
    return (
        jnp.zeros((block.shape[0], 128), jnp.float32).at[target_rows].add(arrived.reshape(-1, 128))
    )


def per_device(model, source, observed, owner_ids, offsets, lengths):
    block = model[:, 0, :]
    masks = layer_masks(LY)
    owners_count = lax.axis_size("mdl")
    capacity = max(4, 2 * source.shape[0] * LZ // owners_count)
    block_partial = settle(
        block, source, observed, owner_ids, offsets, lengths, owners_count, capacity, masks
    )
    share = block.shape[0] // lax.axis_size("grp")
    mine = lax.psum_scatter(block_partial, "grp", scatter_dimension=0, tiled=True)
    local_model = lax.dynamic_slice_in_dim(block, lax.axis_index("grp") * share, share, 0)
    return (mine + smoothing(local_model))[:, None, :]


def solution(mesh):
    placed = (
        P(None, "mdl", None),
        P(("grp", "mdl"), None, None, None),
        P(("grp", "mdl"), None, None, None),
        P(("grp", "mdl"), None, None),
        P(("grp", "mdl"), None),
        P(("grp", "mdl"), None),
    )
    return jax.shard_map(
        per_device, mesh=mesh, in_specs=placed, out_specs=P("grp", "mdl", None), check_vma=False
    )
```

profile of v0, /device:TPU:1, one launch (start us, length us, event | category | flops | bytes accessed | tf_op | source)
XLA Modules:
  0.0 386.6 jit_solution(10517994230864086313)
XLA Ops:
  6.5 0.5 broadcast.389
  7.0 1.5 fusion.35
  8.7 0.2 select_reduce_fusion
  9.0 0.8 reshape.187
  9.7 0.6 scatter_custom_fusion
  10.4 0.7 all_to_all.13
  11.0 10.1 %all-to-all-start = ((s32[8,1,4]{2,1,0:T(1,128)}), s32[8,1,4]{2,1,0:T(1,128)S(1)}, u32[]{:S(2)}, u32[]{:S(2)}) async-start(s32[8,1,4]{2,1,0:T(1,128)} %bitcast.2), calls=%async_computation | async-start | bytes 8192 | tf_op jit(solution)/shard_map/all_to_all | solution.py:117
  21.2 0.8 lt.118
  22.1 7.9 %all-to-all-done = s32[8,1,4]{2,1,0:T(1,128)S(1)} async-done(((s32[8,1,4]{2,1,0:T(1,128)}), s32[8,1,4]{2,1,0:T(1,128)S(1)}, u32[]{:S(2)}, u32[]{:S(2)}) %all-to-all-start) | async-done | bytes 160 | tf_op jit(solution)/shard_map/all_to_all | solution.py:117
  30.2 2.8 gather_fusion
  33.0 0.9 exp.4
  33.9 4.3 %all-to-all-start.1 = ((f32[8,4,32,128]{3,2,1,0:T(8,128)}), f32[8,4,32,128]{3,2,1,0:T(8,128)}, u32[]{:S(2)}, u32[]{:S(2)}) async-start(f32[8,4,32,128]{3,2,1,0:T(8,128)} %bitcast.246), calls=%async_computation.1 | async-start | bytes 1048576 | tf_op jit(solution)/shard_map/all_to_all | solution.py:106
  38.4 11.0 %all-to-all-done.1 = f32[8,4,32,128]{3,2,1,0:T(8,128)} async-done(((f32[8,4,32,128]{3,2,1,0:T(8,128)}), f32[8,4,32,128]{3,2,1,0:T(8,128)}, u32[]{:S(2)}, u32[]{:S(2)}) %all-to-all-start.1) | async-done | bytes 524320 | tf_op jit(solution)/shard_map/all_to_all | solution.py:106
  49.4 1.6 gather_fusion.1
  51.0 0.7 copy-done.2
  51.7 0.8 broadcast_select_fusion
  52.5 1.0 select_n.116
  54.0 0.1 slice.403
  54.1 0.1 slice.410
  54.3 0.1 slice.406
  54.4 0.1 subtract_subtract_fusion.16
  54.6 0.3 subtract_bitcast_fusion.17
  54.9 0.2 fusion.4
  55.4 0.1 slice.418
  55.5 0.1 slice.425
  55.7 0.1 slice.421
  55.8 0.1 subtract_subtract_fusion.13
  56.0 0.3 subtract_bitcast_fusion.14
  56.3 0.3 copy_add_fusion.2
  56.9 0.1 slice.433
  57.0 0.1 slice.440
  57.2 0.1 slice.436
  57.4 0.2 subtract_subtract_fusion.10
  57.5 0.3 subtract_bitcast_fusion.11
  57.9 0.8 copy-done.4
  58.7 0.3 fusion.36
  58.9 0.1 subtract_multiply_fusion
  59.3 0.1 slice.448
  59.4 0.1 slice.455
  59.6 0.1 slice.451
  59.7 0.1 subtract_subtract_fusion.7
  59.9 0.3 subtract_bitcast_fusion.8
  60.2 0.2 fusion.9
  60.7 0.1 slice.463
  60.8 0.1 slice.470
  61.0 0.1 slice.466
  61.2 0.1 subtract_subtract_fusion.4
  61.3 0.3 subtract_bitcast_fusion.5
  61.6 0.4 fusion.12
  62.2 0.1 slice.478
  62.4 0.1 slice.485
  62.5 0.1 slice.481
  62.7 0.2 subtract_subtract_fusion.1
  62.9 0.3 subtract_bitcast_fusion.2
  63.2 0.3 fusion.14
  63.6 0.6 copy-done.3
  64.2 0.2 fusion.19
  64.4 0.9 broadcast_in_dim.18
  65.2 2.5 scatter_fusion
  67.7 3.5 all-to-all-start.2
  71.4 10.9 %all-to-all-done.2 = f32[8,4,32,128]{3,2,1,0:T(8,128)S(1)} async-done(((f32[8,4,32,128]{3,2,1,0:T(8,128)}), f32[8,4,32,128]{3,2,1,0:T(8,128)S(1)}, u32[]{:S(2)}, u32[]{:S(2)}) %all-to-all-start.2) | async-done | bytes 524320 | tf_op jit(solution)/shard_map/all_to_all | solution.py:116
  82.3 7.4 %scatter_custom_fusion.2 = f32[4096,128]{1,0:T(8,128)} fusion(s32[1024]{0:T(1024)S(1)} %bitcast.254, f32[1024,128]{1,0:T(8,128)S(1)} %bitcast.251, f32[]{:T(128)} %constant.18.clone.1), kind=kCustom, calls=%fused_computation.5 | custom fusion | flops 131072 | bytes 2097156 | tf_op jit(solution)/shard_map/scatter-add | solution.py:121
  89.9 288.4 %reduce-scatter.2.cloned.1.call-done = f32[64,128]{1,0:T(8,128)} async-done(((f32[4096,128]{1,0:T(8,128)}), f32[64,128]{1,0:T(8,128)}) %reduce-scatter.2.cloned.1.call-update) | async-done | bytes 32784 | tf_op jit(solution)/shard_map/reduce_scatter | solution.py:134
  378.3 1.5 fusion.22
  (63 shorter events, 2.9 us)
Async XLA Ops:
  6.5 23.6 %copy-start = (f32[4096,1,128]{2,1,0:T(1,128)S(1)}, f32[4096,1,128]{2,1,0:T(1,128)}, u32[]{:S(2)}) copy-start(f32[4096,1,128]{2,1,0:T(1,128)} %param.6) | copy-start | bytes 6291460
  11.0 18.9 %all-to-all-start = ((s32[8,1,4]{2,1,0:T(1,128)}), s32[8,1,4]{2,1,0:T(1,128)S(1)}, u32[]{:S(2)}, u32[]{:S(2)}) async-start(s32[8,1,4]{2,1,0:T(1,128)} %bitcast.2), calls=%async_computation | async-start | bytes 8192 | tf_op jit(solution)/shard_map/all_to_all | solution.py:117
  33.9 19.8 %copy-start.1 = (f32[2,3,8,4096]{3,2,1,0:T(8,128)S(1)}, f32[2,3,8,4096]{3,2,1,0:T(8,128)}, u32[]{:S(2)}) copy-start(f32[2,3,8,4096]{3,2,1,0:T(8,128)} %param.7) | copy-start | bytes 2359300
  33.9 15.5 %all-to-all-start.1 = ((f32[8,4,32,128]{3,2,1,0:T(8,128)}), f32[8,4,32,128]{3,2,1,0:T(8,128)}, u32[]{:S(2)}, u32[]{:S(2)}) async-start(f32[8,4,32,128]{3,2,1,0:T(8,128)} %bitcast.246), calls=%async_computation.1 | async-start | bytes 1048576 | tf_op jit(solution)/shard_map/all_to_all | solution.py:106
  51.0 0.7 copy-start.2
  57.5 1.1 copy-start.4
  63.2 1.0 copy-start.3
  67.7 14.6 %all-to-all-start.2 = ((f32[8,4,32,128]{3,2,1,0:T(8,128)}), f32[8,4,32,128]{3,2,1,0:T(8,128)S(1)}, u32[]{:S(2)}, u32[]{:S(2)}) async-start(f32[8,4,32,128]{3,2,1,0:T(8,128)} %bitcast.44), calls=%async_computation.2 | async-start | bytes 1048576 | tf_op jit(solution)/shard_map/all_to_all | solution.py:116
  71.2 307.1 %reduce-scatter.2.cloned.1.call-start = ((), (), s32[]{:S(2)}) async-start(), calls=%async_computation.4 | async-start | bytes 2129920 | tf_op jit(solution)/shard_map/reduce_scatter | solution.py:134
Sparse Core Ops, SparseCore 0:
  89.9 288.3 reduce-scatter.1
where the time goes:
time: 392 us; the launch traced here: 387 us
  waiting for transfers between devices  318 us (81%)
  local copies, waits for them, and re-layouts  19.5 us (5%)
  starting transfers between devices  17.9 us (5%)
  other arithmetic  17.1 us (4%)
  between operations  14 us (4%)
    reduce_scatter x1, waiting for transfers between devices, per_device(): lax.psum_scatter(block_partial, 'grp', scatter_dimension=0, tiled=True)  288 us
    all_to_all x1, waiting for transfers between devices, settle(): lax.all_to_all(values, 'mdl', split_axis=0, concat_axis=0, tiled=True)  11 us
    all_to_all x1, waiting for transfers between devices, settle(): lax.all_to_all(outgoing, 'mdl', split_axis=0, concat_axis=0, tiled=True)  10.9 us
    all_to_all x1, starting transfers between devices, settle(): lax.all_to_all(request, 'mdl', split_axis=0, concat_axis=0, tiled=True)  10.1 us
    all_to_all x1, waiting for transfers between devices, settle(): lax.all_to_all(request, 'mdl', split_axis=0, concat_axis=0, tiled=True)  7.9 us
  transfers between devices with their start and end apart: 4, of which 4 were waited for; matrix products, arithmetic and copies ran while one was open for 0% of the time, Pallas kernels for 0%

commit v1 on v0

v1 whole, which is shorter than its diff:
```python
import functools

import jax
import jax.numpy as jnp
from jax import lax
from jax.experimental import pallas as pl
from jax.experimental.pallas import tpu as pltpu
from jax.sharding import PartitionSpec as P

LZ = 8
S_DEV = 2
TILES = S_DEV * LZ
TILE = 32
ROWS = 4096
CAP = 4
AIR = 0.05
BETA = 0.5

NZ, NY, NX = 8, 4, 4
OWN = 2 * NX
SLOT_ROWS = CAP * TILE
SHARE = ROWS // (NZ * NY * 2)

MESH = pl.DeviceIdType.MESH
SMEM = pl.BlockSpec(memory_space=pltpu.SMEM)
VMEM = pl.BlockSpec(memory_space=pltpu.VMEM)
FAR_FIRST = [(1, 2), (1, 1), (1, 3), (1, 0), (0, 2), (0, 1), (0, 3)]


def here():
    g, m = lax.axis_index("grp"), lax.axis_index("mdl")
    return g // (2 * NY), (g // 2) % NY, g % 2, m // NX, m % NX


def partner(dh, dx):
    z, y, c, h, x = here()
    y = NY - 1 - y if dh % 2 else y
    m = ((h + dh) % 2) * NX + (x + dx) % NX
    return ((z * NY + y) * 2 + c, m), m


def other_core():
    z, y, c, h, x = here()
    return ((z * NY + y) * 2 + 1 - c, h * NX + x)


def meet(ids):
    barrier = pltpu.get_barrier_semaphore()
    for i in ids:
        pl.semaphore_signal(barrier, inc=1, device_id=i, device_id_type=MESH)
    pl.semaphore_wait(barrier, len(ids))


def remote(src, dst, send, recv, to):
    return pltpu.make_async_remote_copy(
        src_ref=src, dst_ref=dst, send_sem=send, recv_sem=recv, device_id=to, device_id_type=MESH
    )


def tables_kernel(owner, offset, place, request, counts):
    for o in range(OWN):
        counts[o] = 0
        for k in range(CAP):
            request[o, k] = 0
    for t in range(TILES):
        o = owner[t // LZ, t % LZ, 0]
        k = counts[o]
        counts[o] = k + 1
        place[t] = o * CAP + k
        request[o, k] = offset[t // LZ, t % LZ]


def fetch_kernel(request, block, values, starts, outbox, ask_send, ask_recv, row_send, row_recv, core_sem):
    me = lax.axis_index("mdl")
    meet([partner(*d)[0] for d in FAR_FIRST] + [other_core()])
    asks, answers = {}, {}
    for dh, dx in FAR_FIRST:
        to, m = partner(dh, dx)
        k = dh * NX + dx
        asks[dh, dx] = remote(request.at[m], starts.at[0, me], ask_send.at[k], ask_recv.at[k], to)
        asks[dh, dx].start()
    for k in range(CAP):
        starts[0, me, k] = request[me, k]
        values[me, pl.ds(k * TILE, TILE), :] = block[pl.ds(request[me, k], TILE), :]
    for dh, dx in FAR_FIRST:
        back = (-dh % 2, -dx % NX)
        asks[back].wait_recv()
        to, m = partner(dh, dx)
        k = dh * NX + dx
        for i in range(CAP):
            outbox[k, pl.ds(i * TILE, TILE), :] = block[pl.ds(starts[0, m, i], TILE), :]
        answers[dh, dx] = remote(outbox.at[k], values.at[me], row_send.at[k], row_recv.at[k], to)
        answers[dh, dx].start()
    pass_on = remote(starts.at[0], starts.at[1], core_sem.at[0], core_sem.at[1], other_core())
    pass_on.start()
    for d in FAR_FIRST:
        asks[d].wait_send()
        answers[d].wait()
    pass_on.wait()


def solve_kernel(place, lengths, values, source, observed, out, cond, weight, state, rhs, field, part):
    lane = lax.broadcasted_iota(jnp.int32, (8, 128), 1)
    layer = lax.broadcasted_iota(jnp.int32, (8, 128), 0)
    low = lane < 64
    y_next, y_prev = lane % 64 != 63, lane % 64 != 0
    z_next, z_prev = layer != LZ - 1, layer != 0
    row = lax.broadcasted_iota(jnp.int32, (TILE, 128), 0)
    zero = jnp.zeros((8, 128), jnp.float32)

    def half(v):
        return pltpu.roll(v, 64, 1)

    def y_up(v):
        return jnp.where(y_next, pltpu.roll(v, 127, 1), 0.0)

    def y_down(v):
        return jnp.where(y_prev, pltpu.roll(v, 1, 1), 0.0)

    def z_up(v):
        return jnp.where(z_next, pltpu.roll(v, 7, 0), 0.0)

    def z_down(v):
        return jnp.where(z_prev, pltpu.roll(v, 1, 0), 0.0)

    for t in range(TILES):
        s, z = t // LZ, t % LZ
        got = values[pl.ds(pl.multiple_of(place[t] * TILE, TILE), TILE), :]
        cond[s, pl.ds(z, TILE, stride=8), :] = jnp.where(row < lengths[s, z], jnp.exp(got), AIR)

    def split(a, b):
        return jnp.where(low, a, half(b)), jnp.where(low, half(a), b)

    def tile(k):
        return pl.ds(pl.multiple_of(k * 128, 128), 128)

    def weigh(k, carry):
        for s in range(S_DEV):
            here_, there = (cond[s, pl.ds(pl.multiple_of((k + d) * 8, 8), 8), :] for d in (0, 16))
            for i, c in enumerate(split(here_, there)):
                w = 0.5 / (4.0 + c)
                weight[s, 2 * k + i] = w
            for a in range(3):
                pair = split(source[s, a, :, tile(k)], source[s, a, :, tile(k + 16)])
                for i, v in enumerate(pair):
                    b = weight[s, 2 * k + i] * v
                    rhs[s, a, 2 * k + i] = b
                    state[s, a, 2 * k + i] = b
        return carry

    lax.fori_loop(0, 16, weigh, 0, unroll=2)

    def curl(e, e_x):
        ex, ey, ez = e
        hx = (y_up(ez) - ez) - (z_up(ey) - ey)
        hy = (z_up(ex) - ex) - (e_x[2] - ez)
        hz = (e_x[1] - ey) - (y_up(ex) - ex)
        return hx, hy, hz

    def sweep(state, step_rhs):
        def at(s, r):
            return [state[s, a, r] for a in range(3)]

        first, before = [], []
        for s in range(S_DEV):
            ends = [jnp.where(low, half(v), 0.0) for v in at(s, 0)]
            for a in range(3):
                state[s, a, TILE] = ends[a]
            _, hy, hz = curl(at(s, TILE - 1), ends)
            first.append(tuple(at(s, 0)))
            before.append(tuple(jnp.where(low, 0.0, half(v)) for v in (hy, hz)))

        def body(r, carry):
            now, last = carry
            nexts, lasts = [], []
            for s in range(S_DEV):
                e = now[s]
                e_x = tuple(at(s, r + 1))
                hx, hy, hz = curl(e, e_x)
                hy_x, hz_x = last[s]
                back = (
                    (z_down(hy) - hy) - (y_down(hz) - hz),
                    (hz_x - hz) - (z_down(hx) - hx),
                    (y_down(hx) - hx) - (hy_x - hy),
                )
                w = weight[s, r]
                keep = 0.5 + 4.0 * w
                for a in range(3):
                    state[s, a, r] = keep * e[a] + (step_rhs[s, a, r] - w * back[a])
                nexts.append(e_x)
                lasts.append((hy, hz))
            return tuple(nexts), tuple(lasts)

        lax.fori_loop(0, TILE, body, (tuple(first), tuple(before)), unroll=2)

    def sweeps(state):
        def one(i, carry):
            sweep(state, rhs)
            return carry

        lax.fori_loop(0, 3, one, 0)

    sweeps(state)

    def misfit(k, carry):
        for s in range(S_DEV):
            for a in range(3):
                pair = split(observed[s, a, :, tile(k)], observed[s, a, :, tile(k + 16)])
                for i, v in enumerate(pair):
                    b = weight[s, 2 * k + i] * (state[s, a, 2 * k + i] - v)
                    rhs[s, a, 2 * k + i] = b
                    field[s, a, 2 * k + i] = b
        return carry

    lax.fori_loop(0, 16, misfit, 0, unroll=2)
    sweeps(field)

    def products(k, carry):
        for s in range(S_DEV):
            p, q = (
                sum(state[s, a, 2 * k + i] * field[s, a, 2 * k + i] for a in range(3)) for i in range(2)
            )
            for d, v in ((0, jnp.where(low, p, half(q))), (16, jnp.where(low, half(p), q))):
                at = pl.ds(pl.multiple_of((k + d) * 8, 8), 8)
                part[s, at, :] = -cond[s, at, :] * v
        return carry

    lax.fori_loop(0, 16, products, 0, unroll=2)

    out[...] = jnp.zeros_like(out)
    for t in range(TILES):
        s, z = t // LZ, t % LZ
        got = part[s, pl.ds(z, TILE, stride=8), :]
        out[pl.ds(pl.multiple_of(place[t] * TILE, TILE), TILE), :] = jnp.where(row < lengths[s, z], got, 0.0)


def send_kernel(slots, arrived, send, recv, core_send, core_recv, own_sem):
    me = lax.axis_index("mdl")
    meet([partner(*d)[0] for d in FAR_FIRST] + [other_core()])
    copies, forwards = {}, []
    for dh, dx in FAR_FIRST:
        to, m = partner(dh, dx)
        k = dh * NX + dx
        copies[dh, dx] = remote(slots.at[m], arrived.at[0, me], send.at[k], recv.at[k], to)
        copies[dh, dx].start()
    own = pltpu.make_async_copy(slots.at[me], arrived.at[0, me], own_sem)
    own.start()
    forwards.append(remote(slots.at[me], arrived.at[1, me], core_send.at[0], core_recv.at[0], other_core()))
    forwards[0].start()
    for dh, dx in FAR_FIRST[::-1]:
        _, m = partner(dh, dx)
        back = (-dh % 2, -dx % NX)
        copies[back].wait_recv()
        k = dh * NX + dx
        forwards.append(
            remote(arrived.at[0, m], arrived.at[1, m], core_send.at[k], core_recv.at[k], other_core())
        )
        forwards[-1].start()
    own.wait()
    for d in FAR_FIRST:
        copies[d].wait_send()
    for f in forwards:
        f.wait()


def add_kernel(starts, arrived, total):
    total[...] = jnp.zeros_like(total)
    for side in range(2):
        for m in range(OWN):
            for k in range(CAP):
                at = pl.ds(starts[side, m, k], TILE)
                total[at, :] += arrived[side, m, pl.ds(k * TILE, TILE), :]


PIECE = SHARE // 2


def reduce_kernel(total, model, out, up, down, final, spread, up_sem, down_sem, y_send, y_recv):
    z, y, c, h, x = here()
    m = lax.axis_index("mdl")
    above = ((((z + 1) % NZ) * NY + y) * 2 + c, m)
    below = ((((z + NZ - 1) % NZ) * NY + y) * 2 + c, m)
    others = [((z * NY + (y + d) % NY) * 2 + c, m) for d in range(1, NY)]
    meet([above, below] + others)

    def own(d, way):
        return total.at[d, :, c, pl.ds(way * PIECE, PIECE), :]

    rings = (
        (up, up_sem, above, lambda s: (z + 2 * NZ - 1 - s) % NZ),
        (down, down_sem, below, lambda s: (z + 1 + s) % NZ),
    )
    flights = []
    for s in range(NZ):
        for way, (box, sem, to, chunk) in enumerate(rings):
            if s:
                flights[2 * (s - 1) + way].wait_recv()
            if s < NZ - 1:
                if s:
                    box[s - 1] += total[chunk(s), :, c, pl.ds(way * PIECE, PIECE), :]
                    src = box.at[s - 1]
                else:
                    src = own(chunk(0), way)
                flights.append(remote(src, box.at[s], sem.at[0, s], sem.at[1, s], to))
                flights[-1].start()
            else:
                final[:, pl.ds(way * PIECE, PIECE), :] = (
                    box[s - 1] + total[z, :, c, pl.ds(way * PIECE, PIECE), :]
                )
    sends = []
    for d in range(1, NY):
        sends.append(
            remote(final.at[(y + d) % NY], spread.at[d - 1], y_send.at[d - 1], y_recv.at[d - 1], others[d - 1])
        )
        sends[-1].start()
    mine = model[...]
    lane = lax.broadcasted_iota(jnp.int32, (SHARE, 128), 1)
    left = jnp.where(lane == 0, mine, pltpu.roll(mine, 1, 1))
    right = jnp.where(lane == 127, mine, pltpu.roll(mine, 127, 1))
    acc = final[y] + BETA * (2.0 * mine - left - right)
    for d in range(1, NY):
        sends[d - 1].wait()
        acc = acc + spread[d - 1]
    out[...] = acc
    for f in flights:
        f.wait_send()


def per_device(model, source, observed, owner_ids, offsets, lengths):
    block = model.reshape(ROWS, 128)
    f32, i32 = jnp.float32, jnp.int32
    dma = pltpu.SemaphoreType.DMA
    place, request = pl.pallas_call(
        tables_kernel,
        out_shape=(jax.ShapeDtypeStruct((TILES,), i32), jax.ShapeDtypeStruct((OWN, 128), i32)),
        in_specs=[SMEM, SMEM],
        out_specs=(SMEM, SMEM),
        scratch_shapes=[pltpu.SMEM((OWN,), i32)],
        name="tables",
    )(owner_ids, offsets)
    values, starts = pl.pallas_call(
        fetch_kernel,
        out_shape=(
            jax.ShapeDtypeStruct((OWN, SLOT_ROWS, 128), f32),
            jax.ShapeDtypeStruct((2, OWN, 128), i32),
        ),
        in_specs=[SMEM, VMEM],
        out_specs=(VMEM, SMEM),
        scratch_shapes=[pltpu.VMEM((OWN, SLOT_ROWS, 128), f32)] + [dma((OWN,))] * 4 + [dma((2,))],
        compiler_params=pltpu.CompilerParams(collective_id=0, has_side_effects=True),
        name="fetch",
    )(request, block)
    slots = pl.pallas_call(
        solve_kernel,
        out_shape=jax.ShapeDtypeStruct((OWN * SLOT_ROWS, 128), f32),
        in_specs=[SMEM, SMEM, VMEM, VMEM, VMEM],
        out_specs=VMEM,
        scratch_shapes=[
            pltpu.VMEM((S_DEV, TILE * 8, 128), f32),
            pltpu.VMEM((S_DEV, TILE, 8, 128), f32),
            pltpu.VMEM((S_DEV, 3, TILE + 1, 8, 128), f32),
            pltpu.VMEM((S_DEV, 3, TILE, 8, 128), f32),
            pltpu.VMEM((S_DEV, 3, TILE + 1, 8, 128), f32),
            pltpu.VMEM((S_DEV, TILE * 8, 128), f32),
        ],
        compiler_params=pltpu.CompilerParams(vmem_limit_bytes=32 << 20),
        name="solve",
    )(place, lengths, values.reshape(OWN * SLOT_ROWS, 128), source, observed)
    arrived = pl.pallas_call(
        send_kernel,
        out_shape=jax.ShapeDtypeStruct((2, OWN, SLOT_ROWS, 128), f32),
        in_specs=[VMEM],
        out_specs=VMEM,
        scratch_shapes=[dma((OWN,))] * 4 + [dma],
        compiler_params=pltpu.CompilerParams(collective_id=1, has_side_effects=True),
        name="send",
    )(slots.reshape(OWN, SLOT_ROWS, 128))
    total = pl.pallas_call(
        add_kernel,
        out_shape=jax.ShapeDtypeStruct((ROWS, 128), f32),
        in_specs=[SMEM, VMEM],
        out_specs=VMEM,
        compiler_params=pltpu.CompilerParams(vmem_limit_bytes=32 << 20),
        name="add",
    )(starts, arrived)
    mine = lax.dynamic_slice_in_dim(block, lax.axis_index("grp") * SHARE, SHARE, 0)
    gradient = pl.pallas_call(
        reduce_kernel,
        out_shape=jax.ShapeDtypeStruct((SHARE, 128), f32),
        in_specs=[VMEM, VMEM],
        out_specs=VMEM,
        scratch_shapes=[
            pltpu.VMEM((NZ - 1, NY, PIECE, 128), f32),
            pltpu.VMEM((NZ - 1, NY, PIECE, 128), f32),
            pltpu.VMEM((NY, SHARE, 128), f32),
            pltpu.VMEM((NY - 1, SHARE, 128), f32),
            dma((2, NZ - 1)),
            dma((2, NZ - 1)),
            dma((NY - 1,)),
            dma((NY - 1,)),
        ],
        compiler_params=pltpu.CompilerParams(
            collective_id=2, has_side_effects=True, vmem_limit_bytes=32 << 20
        ),
        name="reduce",
    )(total.reshape(NZ, NY, 2, SHARE, 128), mine)
    return gradient[:, None, :]


def solution(mesh):
    placed = (
        P(None, "mdl", None),
        P(("grp", "mdl"), None, None, None),
        P(("grp", "mdl"), None, None, None),
        P(("grp", "mdl"), None, None),
        P(("grp", "mdl"), None),
        P(("grp", "mdl"), None),
    )
    return jax.shard_map(
        per_device, mesh=mesh, in_specs=placed, out_specs=P("grp", "mdl", None), check_vma=False
    )
```

time: 392 us -> 108 us (0.28)
  the two profiles are of different devices: /device:TPU:1 before, /device:TPU:8 now
where the time goes in v1:
time: 108 us; the launch traced here: 107 us
  Pallas kernels  101 us (94%)
  local copies, waits for them, and re-layouts  5.94 us (6%)
    pallas_call x1, Pallas kernels, per_device(): pl.pallas_call(reduce_kernel, out_shape=jax.ShapeDtypeStruct((SHARE, 128)...  42.5 us
    pallas_call x1, Pallas kernels, per_device(): pl.pallas_call(fetch_kernel, out_shape=(jax.ShapeDtypeStruct((OWN, SLOT_R...  22.5 us
    pallas_call x1, Pallas kernels, per_device(): pl.pallas_call(solve_kernel, out_shape=jax.ShapeDtypeStruct((OWN * SLOT_R...  18.5 us
    pallas_call x1, Pallas kernels, per_device(): pl.pallas_call(send_kernel, out_shape=jax.ShapeDtypeStruct((2, OWN, SLOT_...  15 us
    unnamed x18, local copies, waits for them, and re-layouts  5.18 us

profile of v1, /device:TPU:8, one launch (start us, length us, event | category | flops | bytes accessed | tf_op | source)
XLA Modules:
  0.0 107.2 jit_solution(8172557817083481388)
XLA Ops:
  0.0 0.0 copy-start.6
  0.0 0.0 copy-start.2
  0.0 0.0 copy-start.3
  0.0 1.5 %copy.7.owner = s32[2,8,1]{2,1,0:T(8,128)} copy(s32[2,8,1]{1,2,0:T(1,128)} %param.9) | data formatting | bytes 128 | tf_op args[3]
  1.5 1.5 %tables.1 = (s32[16]{0:T(128)}, s32[8,128]{1,0:T(8,128)}) custom-call(s32[2,8,1]{2,1,0:T(8,128)} %copy.7.owner, s32[2,8]{1,0:T(2,128)} %offset.1), custom_call_target="tpu_custom_call" | custom-call | tf_op jit(solution)/shard_map/tables/pallas_call | solution.py:333
  3.0 0.0 copy-start.7
  3.0 22.5 %fetch.1 = (f32[8,128,128]{2,1,0:T(8,128)}, s32[2,8,128]{2,1,0:T(8,128)}) custom-call(s32[8,128]{1,0:T(8,128)} %get-tuple-element.9.request, f32[4096,128]{1,0:T(8,128)} %bitcast.13), custom_call_target="tpu_custom_call" | custom-call | tf_op jit(solution)/shard_map/fetch/pallas_call | solution.py:341
  25.6 0.0 copy-done.6
  25.6 0.0 copy-done.2
  25.6 0.0 copy-done.3
  25.6 0.0 copy-done.7
  25.6 0.0 copy-start.4
  25.6 1.0 copy-done.4
  26.7 0.0 copy-start.5
  26.7 18.5 %solve.1 = f32[1024,128]{1,0:T(8,128)S(1)} custom-call(s32[16]{0:T(128)S(1)} %copy-done.7, s32[2,8]{1,0:T(2,128)S(1)} %copy-done.6, f32[1024,128]{1,0:T(8,128)S(1)} %bitcast.10, f32[2,3,8,4096]{3,2,1,0:T(8,128)S(1)} %copy-done.2, f32[2,3,8,4096]{3,2,1,0:T(8,128)S(1)} %copy-done.3), custom_call_target="tpu_custom_call" | custom-call | tf_op jit(solution)/shard_map/solve/pallas_call | solution.py:353
  45.1 0.0 copy-start.1
  45.2 0.8 copy-done.1
  46.0 15.0 %send.1.arrived = f32[2,8,128,128]{3,2,1,0:T(8,128)} custom-call(f32[8,128,128]{2,1,0:T(8,128)} %bitcast.9), custom_call_target="tpu_custom_call" | custom-call | tf_op jit(solution)/shard_map/send/pallas_call | solution.py:369
  61.0 0.0 copy-done.5
  61.0 0.0 copy-start
  61.0 1.2 %copy-done = f32[2,8,128,128]{3,2,1,0:T(8,128)S(1)} copy-done((f32[2,8,128,128]{3,2,1,0:T(8,128)S(1)}, f32[2,8,128,128]{3,2,1,0:T(8,128)}, u32[]{:S(2)}) %copy-start) | copy-done | bytes 1048600
  62.2 1.1 %add.5 = f32[4096,128]{1,0:T(8,128)S(1)} custom-call(s32[2,8,128]{2,1,0:T(8,128)S(1)} %copy-done.5, f32[2,8,128,128]{3,2,1,0:T(8,128)S(1)} %copy-done), custom_call_target="tpu_custom_call" | custom-call | tf_op jit(solution)/shard_map/add/pallas_call | solution.py:378
  63.4 0.8 constant_dynamic-slice_fusion
  64.1 42.5 %reduce.1 = f32[64,128]{1,0:T(8,128)S(1)} custom-call(f32[8,4,2,64,128]{4,3,2,1,0:T(8,128)S(1)} %bitcast.8, f32[64,128]{1,0:T(8,128)S(1)} %bitcast.11), custom_call_target="tpu_custom_call" | custom-call | tf_op jit(solution)/shard_map/reduce/pallas_call | solution.py:387
  106.6 0.6 copy.10
Async XLA Ops:
  0.0 25.6 %copy-start.6 = (s32[2,8]{1,0:T(2,128)S(1)}, s32[2,8]{1,0:T(2,128)}, u32[]{:S(2)}) copy-start(s32[2,8]{1,0:T(2,128)} %lengths.1) | copy-start | bytes 196
  0.0 25.6 %copy-start.2 = (f32[2,3,8,4096]{3,2,1,0:T(8,128)S(1)}, f32[2,3,8,4096]{3,2,1,0:T(8,128)}, u32[]{:S(2)}) copy-start(f32[2,3,8,4096]{3,2,1,0:T(8,128)} %source.1) | copy-start | bytes 2359300
  0.0 25.6 %copy-start.3 = (f32[2,3,8,4096]{3,2,1,0:T(8,128)S(1)}, f32[2,3,8,4096]{3,2,1,0:T(8,128)}, u32[]{:S(2)}) copy-start(f32[2,3,8,4096]{3,2,1,0:T(8,128)} %observed.1) | copy-start | bytes 2359300
  3.0 22.6 %copy-start.7 = (s32[16]{0:T(128)S(1)}, s32[16]{0:T(128)}, u32[]{:S(2)}) copy-start(s32[16]{0:T(128)} %get-tuple-element.11.place) | copy-start | bytes 196
  25.6 1.0 copy-start.4
  26.7 34.3 %copy-start.5 = (s32[2,8,128]{2,1,0:T(8,128)S(1)}, s32[2,8,128]{2,1,0:T(8,128)}, u32[]{:S(2)}) copy-start(s32[2,8,128]{2,1,0:T(8,128)} %get-tuple-element.10.starts) | copy-start | bytes 24580
  45.1 0.8 copy-start.1
  61.0 1.2 %copy-start = (f32[2,8,128,128]{3,2,1,0:T(8,128)S(1)}, f32[2,8,128,128]{3,2,1,0:T(8,128)}, u32[]{:S(2)}) copy-start(f32[2,8,128,128]{3,2,1,0:T(8,128)} %send.1.arrived) | copy-start | bytes 3145732

commit v2 on v1

v2 whole, which is shorter than its diff:
```python
import functools

import jax
import jax.numpy as jnp
from jax import lax
from jax.experimental import pallas as pl
from jax.experimental.pallas import tpu as pltpu
from jax.sharding import PartitionSpec as P

LZ = 8
S_DEV = 2
TILES = S_DEV * LZ
TILE = 32
ROWS = 4096
CAP = 4
AIR = 0.05
BETA = 0.5

NZ, NY, NX = 8, 4, 4
OWN = 2 * NX
SLOT_ROWS = CAP * TILE
SHARE = ROWS // (NZ * NY * 2)

MESH = pl.DeviceIdType.MESH
SMEM = pl.BlockSpec(memory_space=pltpu.SMEM)
VMEM = pl.BlockSpec(memory_space=pltpu.VMEM)
FAR_FIRST = [(1, 2), (1, 1), (1, 3), (1, 0), (0, 2), (0, 1), (0, 3)]


def here():
    g, m = lax.axis_index("grp"), lax.axis_index("mdl")
    return g // (2 * NY), (g // 2) % NY, g % 2, m // NX, m % NX


def partner(dh, dx):
    z, y, c, h, x = here()
    y = NY - 1 - y if dh % 2 else y
    m = ((h + dh) % 2) * NX + (x + dx) % NX
    return ((z * NY + y) * 2 + c, m), m


def other_core():
    z, y, c, h, x = here()
    return ((z * NY + y) * 2 + 1 - c, h * NX + x)


def meet(ids):
    barrier = pltpu.get_barrier_semaphore()
    for i in ids:
        pl.semaphore_signal(barrier, inc=1, device_id=i, device_id_type=MESH)
    pl.semaphore_wait(barrier, len(ids))


def remote(src, dst, send, recv, to):
    return pltpu.make_async_remote_copy(
        src_ref=src, dst_ref=dst, send_sem=send, recv_sem=recv, device_id=to, device_id_type=MESH
    )


def tables_kernel(owner, offset, place, request, counts):
    for o in range(OWN):
        counts[o] = 0
        for k in range(CAP):
            request[o, k] = 0
    for t in range(TILES):
        o = owner[t // LZ, 0, t % LZ]
        k = counts[o]
        counts[o] = k + 1
        place[t] = o * CAP + k
        request[o, k] = offset[t // LZ, t % LZ]


def fetch_kernel(request, block, values, starts, outbox, ask_send, ask_recv, row_send, row_recv, core_sem):
    me = lax.axis_index("mdl")
    meet([partner(*d)[0] for d in FAR_FIRST] + [other_core()])
    asks, answers = {}, {}
    for dh, dx in FAR_FIRST:
        to, m = partner(dh, dx)
        k = dh * NX + dx
        asks[dh, dx] = remote(request.at[m], starts.at[0, me], ask_send.at[k], ask_recv.at[k], to)
        asks[dh, dx].start()
    for k in range(CAP):
        starts[0, me, k] = request[me, k]
    for dh, dx in FAR_FIRST:
        back = (-dh % 2, -dx % NX)
        asks[back].wait_recv()
        to, m = partner(dh, dx)
        k = dh * NX + dx
        for i in range(CAP):
            outbox[k, pl.ds(i * TILE, TILE), :] = block[pl.ds(starts[0, m, i], TILE), :]
        answers[dh, dx] = remote(outbox.at[k], values.at[me], row_send.at[k], row_recv.at[k], to)
        answers[dh, dx].start()
    pass_on = remote(starts.at[0], starts.at[1], core_sem.at[0], core_sem.at[1], other_core())
    pass_on.start()
    for k in range(CAP):
        values[me, pl.ds(k * TILE, TILE), :] = block[pl.ds(starts[0, me, k], TILE), :]
    for d in FAR_FIRST:
        asks[d].wait_send()
        answers[d].wait()
    pass_on.wait()


BATCH = 4


def solve_kernel(place, lengths, values, source, observed, out, cond, weight, first, second, third, rhs, part):
    lane = lax.broadcasted_iota(jnp.int32, (8, 128), 1)
    layer = lax.broadcasted_iota(jnp.int32, (8, 128), 0)
    low = lane < 64
    y_next, y_prev = lane % 64 != 63, lane % 64 != 0
    z_next, z_prev = layer != LZ - 1, layer != 0
    row = lax.broadcasted_iota(jnp.int32, (TILE, 128), 0)

    def half(v):
        return pltpu.roll(v, 64, 1)

    def shift(mask, by, axis):
        def one(v):
            return jnp.where(mask, pltpu.roll(v, by, axis), 0.0)

        return lambda v: one(v) if v.ndim == 2 else jnp.stack([one(v[i]) for i in range(v.shape[0])])

    y_up, y_down = shift(y_next, 127, 1), shift(y_prev, 1, 1)
    z_up, z_down = shift(z_next, LZ - 1, 0), shift(z_prev, 1, 0)

    for t in range(TILES):
        s, z = t // LZ, t % LZ
        got = values[pl.ds(pl.multiple_of(place[t] * TILE, TILE), TILE), :]
        cond[s, pl.ds(z, TILE, stride=8), :] = jnp.where(row < lengths[s, z], jnp.exp(got), AIR)

    def split(a, b):
        return jnp.where(low, a, half(b)), jnp.where(low, half(a), b)

    def tile(k):
        return pl.ds(k * 128, 128)

    for k in range(TILE // 2):
        for s in range(S_DEV):
            pair = split(*[cond[s, pl.ds((k + d) * 8, 8), :] for d in (0, TILE // 2)])
            ws = [0.5 / (4.0 + c) for c in pair]
            for i in range(2):
                weight[s, 2 * k + i] = ws[i]
            for a in range(3):
                pair = split(source[s, a, :, tile(k)], source[s, a, :, tile(k + TILE // 2)])
                for i in range(2):
                    b = ws[i] * pair[i]
                    rhs[s, a, 2 * k + i] = b
                    first[s, a, 2 * k + i] = b

    def curl(e, e_x):
        ex, ey, ez = e
        hx = (y_up(ez) - ez) - (z_up(ey) - ey)
        hy = (z_up(ex) - ex) - (e_x[2] - ez)
        hz = (e_x[1] - ey) - (y_up(ex) - ex)
        return hx, hy, hz

    def sweep(src, dst):
        before = []
        for s in range(S_DEV):
            ends = [jnp.where(low, half(src[s, a, 0]), 0.0) for a in range(3)]
            for a in range(1, 3):
                src[s, a, TILE] = ends[a]
            _, hy, hz = curl([src[s, a, TILE - 1] for a in range(3)], ends)
            before.append(tuple(jnp.where(low, 0.0, half(v))[None] for v in (hy, hz)))

        def body(b, carry):
            at = pl.ds(b * BATCH, BATCH)
            lasts = []
            for s in range(S_DEV):
                e = [src[s, a, at] for a in range(3)]
                after = pl.ds(b * BATCH + BATCH, 1)
                e_x = [None] + [jnp.concatenate([e[a][1:], src[s, a, after]], 0) for a in (1, 2)]
                hx, hy, hz = curl(e, e_x)
                hy_x = jnp.concatenate([carry[s][0], hy[:-1]], 0)
                hz_x = jnp.concatenate([carry[s][1], hz[:-1]], 0)
                back = (
                    (z_down(hy) - hy) - (y_down(hz) - hz),
                    (hz_x - hz) - (z_down(hx) - hx),
                    (y_down(hx) - hx) - (hy_x - hy),
                )
                w = weight[s, at]
                keep = 0.5 + 4.0 * w
                for a in range(3):
                    dst[s, a, at] = keep * e[a] + (rhs[s, a, at] - w * back[a])
                lasts.append((hy[-1:], hz[-1:]))
            return tuple(lasts)

        lax.fori_loop(0, TILE // BATCH, body, tuple(before), unroll=4)

    sweep(first, second)
    sweep(second, first)
    sweep(first, second)

    for k in range(TILE // 2):
        for s in range(S_DEV):
            for a in range(3):
                pair = split(observed[s, a, :, tile(k)], observed[s, a, :, tile(k + TILE // 2)])
                for i in range(2):
                    b = weight[s, 2 * k + i] * (second[s, a, 2 * k + i] - pair[i])
                    rhs[s, a, 2 * k + i] = b
                    first[s, a, 2 * k + i] = b

    sweep(first, third)
    sweep(third, first)
    sweep(first, third)

    for k in range(TILE // 2):
        for s in range(S_DEV):
            p, q = (
                sum(second[s, a, 2 * k + i] * third[s, a, 2 * k + i] for a in range(3)) for i in range(2)
            )
            for d, v in ((0, jnp.where(low, p, half(q))), (TILE // 2, jnp.where(low, half(p), q))):
                at = pl.ds((k + d) * 8, 8)
                part[s, at, :] = -cond[s, at, :] * v

    out[...] = jnp.zeros_like(out)
    for t in range(TILES):
        s, z = t // LZ, t % LZ
        got = part[s, pl.ds(z, TILE, stride=8), :]
        out[pl.ds(pl.multiple_of(place[t] * TILE, TILE), TILE), :] = jnp.where(row < lengths[s, z], got, 0.0)


def send_kernel(slots, arrived, send, recv, core_send, core_recv, own_sem):
    me = lax.axis_index("mdl")
    meet([partner(*d)[0] for d in FAR_FIRST] + [other_core()])
    copies, forwards = {}, []
    for dh, dx in FAR_FIRST:
        to, m = partner(dh, dx)
        k = dh * NX + dx
        copies[dh, dx] = remote(slots.at[m], arrived.at[0, me], send.at[k], recv.at[k], to)
        copies[dh, dx].start()
    own = pltpu.make_async_copy(slots.at[me], arrived.at[0, me], own_sem)
    own.start()
    forwards.append(remote(slots.at[me], arrived.at[1, me], core_send.at[0], core_recv.at[0], other_core()))
    forwards[0].start()
    for dh, dx in FAR_FIRST[::-1]:
        _, m = partner(dh, dx)
        back = (-dh % 2, -dx % NX)
        copies[back].wait_recv()
        k = dh * NX + dx
        forwards.append(
            remote(arrived.at[0, m], arrived.at[1, m], core_send.at[k], core_recv.at[k], other_core())
        )
        forwards[-1].start()
    own.wait()
    for d in FAR_FIRST:
        copies[d].wait_send()
    for f in forwards:
        f.wait()


def add_kernel(starts, arrived, block, total):
    total[...] = jnp.zeros_like(total)
    at = pl.ds(pl.multiple_of(lax.axis_index("grp") * SHARE, SHARE), SHARE)
    mine = block[at, :]
    lane = lax.broadcasted_iota(jnp.int32, (SHARE, 128), 1)
    left = jnp.where(lane == 0, mine, pltpu.roll(mine, 1, 1))
    right = jnp.where(lane == 127, mine, pltpu.roll(mine, 127, 1))
    total[at, :] = BETA * (2.0 * mine - left - right)
    for side in range(2):
        for m in range(OWN):
            for k in range(CAP):
                at = pl.ds(starts[side, m, k], TILE)
                total[at, :] += arrived[side, m, pl.ds(k * TILE, TILE), :]


PIECE = SHARE // 2


def reduce_kernel(total, out, up, down, final, spread, up_sem, down_sem, y_send, y_recv):
    z, y, c, h, x = here()
    m = lax.axis_index("mdl")
    above = ((((z + 1) % NZ) * NY + y) * 2 + c, m)
    below = ((((z + NZ - 1) % NZ) * NY + y) * 2 + c, m)
    others = [((z * NY + (y + d) % NY) * 2 + c, m) for d in range(1, NY)]
    meet([above, below] + others)

    rings = (
        (up, up_sem, above, lambda s: (z + 2 * NZ - 1 - s) % NZ),
        (down, down_sem, below, lambda s: (z + 1 + s) % NZ),
    )
    order = list(range(1, NY)) + [0]
    flights, sends = {}, {}
    for s in range(NZ):
        for d in order:
            for way, (box, sem, to, chunk) in enumerate(rings):
                rows = pl.ds(way * PIECE, PIECE)
                j = (y + d) % NY
                if s:
                    flights[s - 1, d, way].wait_recv()
                if s == NZ - 1:
                    final[d, rows, :] = box[s - 1, d] + total[z, j, c, rows, :]
                    continue
                src = total.at[chunk(0), j, c, rows, :]
                if s:
                    box[s - 1, d] += total[chunk(s), j, c, rows, :]
                    src = box.at[s - 1, d]
                flights[s, d, way] = remote(src, box.at[s, d], sem.at[0, s, d], sem.at[1, s, d], to)
                flights[s, d, way].start()
            if s == NZ - 1 and d:
                sends[d] = remote(final.at[d], spread.at[d - 1], y_send.at[d - 1], y_recv.at[d - 1], others[d - 1])
                sends[d].start()
    acc = final[0]
    for d in range(1, NY):
        sends[d].wait()
        acc = acc + spread[d - 1]
    out[...] = acc
    for f in flights.values():
        f.wait_send()


def per_device(model, source, observed, owner_ids, offsets, lengths):
    block = model.reshape(ROWS, 128)
    f32, i32 = jnp.float32, jnp.int32
    dma = pltpu.SemaphoreType.DMA
    place, request = pl.pallas_call(
        tables_kernel,
        out_shape=(jax.ShapeDtypeStruct((TILES,), i32), jax.ShapeDtypeStruct((OWN, 128), i32)),
        in_specs=[SMEM, SMEM],
        out_specs=(SMEM, SMEM),
        scratch_shapes=[pltpu.SMEM((OWN,), i32)],
        name="tables",
    )(owner_ids.transpose(0, 2, 1), offsets)
    values, starts = pl.pallas_call(
        fetch_kernel,
        out_shape=(
            jax.ShapeDtypeStruct((OWN, SLOT_ROWS, 128), f32),
            jax.ShapeDtypeStruct((2, OWN, 128), i32),
        ),
        in_specs=[SMEM, VMEM],
        out_specs=(VMEM, SMEM),
        scratch_shapes=[pltpu.VMEM((OWN, SLOT_ROWS, 128), f32)] + [dma((OWN,))] * 4 + [dma((2,))],
        compiler_params=pltpu.CompilerParams(collective_id=0, has_side_effects=True),
        name="fetch",
    )(request, block)
    fields = pltpu.VMEM((S_DEV, 3, TILE + 1, 8, 128), f32)
    slots = pl.pallas_call(
        solve_kernel,
        out_shape=jax.ShapeDtypeStruct((OWN * SLOT_ROWS, 128), f32),
        in_specs=[SMEM, SMEM, VMEM, VMEM, VMEM],
        out_specs=VMEM,
        scratch_shapes=[
            pltpu.VMEM((S_DEV, TILE * 8, 128), f32),
            pltpu.VMEM((S_DEV, TILE, 8, 128), f32),
            fields,
            fields,
            fields,
            pltpu.VMEM((S_DEV, 3, TILE, 8, 128), f32),
            pltpu.VMEM((S_DEV, TILE * 8, 128), f32),
        ],
        compiler_params=pltpu.CompilerParams(vmem_limit_bytes=32 << 20),
        name="solve",
    )(place, lengths, values.reshape(OWN * SLOT_ROWS, 128), source, observed)
    arrived = pl.pallas_call(
        send_kernel,
        out_shape=jax.ShapeDtypeStruct((2, OWN, SLOT_ROWS, 128), f32),
        in_specs=[VMEM],
        out_specs=VMEM,
        scratch_shapes=[dma((OWN,))] * 4 + [dma],
        compiler_params=pltpu.CompilerParams(collective_id=1, has_side_effects=True),
        name="send",
    )(slots.reshape(OWN, SLOT_ROWS, 128))
    total = pl.pallas_call(
        add_kernel,
        out_shape=jax.ShapeDtypeStruct((ROWS, 128), f32),
        in_specs=[SMEM, VMEM, VMEM],
        out_specs=VMEM,
        compiler_params=pltpu.CompilerParams(vmem_limit_bytes=32 << 20),
        name="add",
    )(starts, arrived, block)
    box = pltpu.VMEM((NZ - 1, NY, PIECE, 128), f32)
    gradient = pl.pallas_call(
        reduce_kernel,
        out_shape=jax.ShapeDtypeStruct((SHARE, 128), f32),
        in_specs=[VMEM],
        out_specs=VMEM,
        scratch_shapes=[
            box,
            box,
            pltpu.VMEM((NY, SHARE, 128), f32),
            pltpu.VMEM((NY - 1, SHARE, 128), f32),
            dma((2, NZ - 1, NY)),
            dma((2, NZ - 1, NY)),
            dma((NY - 1,)),
            dma((NY - 1,)),
        ],
        compiler_params=pltpu.CompilerParams(
            collective_id=2, has_side_effects=True, vmem_limit_bytes=32 << 20
        ),
        name="reduce",
    )(total.reshape(NZ, NY, 2, SHARE, 128))
    return gradient[:, None, :]


def solution(mesh):
    placed = (
        P(None, "mdl", None),
        P(("grp", "mdl"), None, None, None),
        P(("grp", "mdl"), None, None, None),
        P(("grp", "mdl"), None, None),
        P(("grp", "mdl"), None),
        P(("grp", "mdl"), None),
    )
    return jax.shard_map(
        per_device, mesh=mesh, in_specs=placed, out_specs=P("grp", "mdl", None), check_vma=False
    )
```

time: 108 us -> 92 us (0.85)
  the two profiles are of different devices: /device:TPU:8 before, /device:TPU:24 now
where the time goes in v2:
time: 92 us; the launch traced here: 91.6 us
  Pallas kernels  86.6 us (94%)
  local copies, waits for them, and re-layouts  4.85 us (5%)
    pallas_call x1, Pallas kernels, per_device(): pl.pallas_call(reduce_kernel, out_shape=jax.ShapeDtypeStruct((SHARE, 128)...  37.6 us
    pallas_call x1, Pallas kernels, per_device(): pl.pallas_call(fetch_kernel, out_shape=(jax.ShapeDtypeStruct((OWN, SLOT_R...  24.7 us
    pallas_call x1, Pallas kernels, per_device(): pl.pallas_call(send_kernel, out_shape=jax.ShapeDtypeStruct((2, OWN, SLOT_...  16 us
    pallas_call x1, Pallas kernels, per_device(): pl.pallas_call(solve_kernel, out_shape=jax.ShapeDtypeStruct((OWN * SLOT_R...  5.6 us
    unnamed x19, local copies, waits for them, and re-layouts  4.85 us

profile of v2, /device:TPU:24, one launch (start us, length us, event | category | flops | bytes accessed | tf_op | source)
XLA Modules:
  0.0 91.6 jit_solution(14962738144792107693)
XLA Ops:
  0.0 0.0 copy-start.7
  0.0 0.0 copy-start.3
  0.0 1.5 %tables.1 = (s32[16]{0:T(128)}, s32[8,128]{1,0:T(8,128)}) custom-call(s32[2,1,8]{2,1,0:T(1,128)} %bitcast.16, s32[2,8]{1,0:T(2,128)} %offset.1), custom_call_target="tpu_custom_call" | custom-call | tf_op jit(solution)/shard_map/tables/pallas_call | solution.py:316
  1.6 0.0 copy-start.8
  1.6 24.7 %fetch.1 = (f32[8,128,128]{2,1,0:T(8,128)}, s32[2,8,128]{2,1,0:T(8,128)}) custom-call(s32[8,128]{1,0:T(8,128)} %get-tuple-element.9.request, f32[4096,128]{1,0:T(8,128)} %bitcast.10), custom_call_target="tpu_custom_call" | custom-call | tf_op jit(solution)/shard_map/fetch/pallas_call | solution.py:324
  26.3 0.0 copy-done.7
  26.3 0.0 copy-done.3
  26.3 0.0 copy-done.8
  26.4 0.0 copy-start.4
  26.4 1.1 %copy-done.4 = f32[2,3,8,4096]{3,2,1,0:T(8,128)S(1)} copy-done((f32[2,3,8,4096]{3,2,1,0:T(8,128)S(1)}, f32[2,3,8,4096]{3,2,1,0:T(8,128)}, u32[]{:S(2)}) %copy-start.4) | copy-done | bytes 786456
  27.5 0.0 copy-start.5
  27.5 1.0 %copy-done.5 = f32[8,128,128]{2,1,0:T(8,128)S(1)} copy-done((f32[8,128,128]{2,1,0:T(8,128)S(1)}, f32[8,128,128]{2,1,0:T(8,128)}, u32[]{:S(2)}) %copy-start.5) | copy-done | bytes 524312
  28.5 0.0 copy-start
  28.5 0.0 copy-start.6
  28.5 5.6 %solve.1 = f32[1024,128]{1,0:T(8,128)S(1)} custom-call(s32[16]{0:T(128)S(1)} %copy-done.8, s32[2,8]{1,0:T(2,128)S(1)} %copy-done.7, f32[1024,128]{1,0:T(8,128)S(1)} %bitcast.14, f32[2,3,8,4096]{3,2,1,0:T(8,128)S(1)} %copy-done.3, f32[2,3,8,4096]{3,2,1,0:T(8,128)S(1)} %copy-done.4), custom_call_target="tpu_custom_call" | custom-call | tf_op jit(solution)/shard_map/solve/pallas_call | solution.py:337
  34.1 0.0 copy-start.2
  34.2 0.8 copy-done.2
  35.0 16.0 %send.1.arrived = f32[2,8,128,128]{3,2,1,0:T(8,128)} custom-call(f32[8,128,128]{2,1,0:T(8,128)} %bitcast.13), custom_call_target="tpu_custom_call" | custom-call | tf_op jit(solution)/shard_map/send/pallas_call | solution.py:354
  51.0 0.0 copy-done
  51.0 0.0 copy-done.6
  51.0 0.0 copy-start.1
  51.0 1.2 %copy-done.1 = f32[2,8,128,128]{3,2,1,0:T(8,128)S(1)} copy-done((f32[2,8,128,128]{3,2,1,0:T(8,128)S(1)}, f32[2,8,128,128]{3,2,1,0:T(8,128)}, u32[]{:S(2)}) %copy-start.1) | copy-done | bytes 1048600
  52.2 1.1 %add.1 = f32[4096,128]{1,0:T(8,128)S(1)} custom-call(s32[2,8,128]{2,1,0:T(8,128)S(1)} %copy-done.6, f32[2,8,128,128]{3,2,1,0:T(8,128)S(1)} %copy-done.1, f32[4096,128]{1,0:T(8,128)S(1)} %bitcast.11), custom_call_target="tpu_custom_call" | custom-call | tf_op jit(solution)/shard_map/add/pallas_call | solution.py:363
  53.3 37.6 %reduce.1 = f32[64,128]{1,0:T(8,128)S(1)} custom-call(f32[8,4,2,64,128]{4,3,2,1,0:T(8,128)S(1)} %bitcast.12), custom_call_target="tpu_custom_call" | custom-call | tf_op jit(solution)/shard_map/reduce/pallas_call | solution.py:372
  91.0 0.6 copy.10
Async XLA Ops:
  0.0 26.3 %copy-start.7 = (s32[2,8]{1,0:T(2,128)S(1)}, s32[2,8]{1,0:T(2,128)}, u32[]{:S(2)}) copy-start(s32[2,8]{1,0:T(2,128)} %lengths.1) | copy-start | bytes 196
  0.0 26.3 %copy-start.3 = (f32[2,3,8,4096]{3,2,1,0:T(8,128)S(1)}, f32[2,3,8,4096]{3,2,1,0:T(8,128)}, u32[]{:S(2)}) copy-start(f32[2,3,8,4096]{3,2,1,0:T(8,128)} %source.1) | copy-start | bytes 2359300
  1.6 24.8 %copy-start.8 = (s32[16]{0:T(128)S(1)}, s32[16]{0:T(128)}, u32[]{:S(2)}) copy-start(s32[16]{0:T(128)} %get-tuple-element.11.place) | copy-start | bytes 196
  26.4 1.1 %copy-start.4 = (f32[2,3,8,4096]{3,2,1,0:T(8,128)S(1)}, f32[2,3,8,4096]{3,2,1,0:T(8,128)}, u32[]{:S(2)}) copy-start(f32[2,3,8,4096]{3,2,1,0:T(8,128)} %observed.1) | copy-start | bytes 2359300
  27.5 1.0 %copy-start.5 = (f32[8,128,128]{2,1,0:T(8,128)S(1)}, f32[8,128,128]{2,1,0:T(8,128)}, u32[]{:S(2)}) copy-start(f32[8,128,128]{2,1,0:T(8,128)} %get-tuple-element.12) | copy-start | bytes 1572868
  28.5 22.5 %copy-start = (f32[4096,1,128]{2,1,0:T(1,128)S(1)}, f32[4096,1,128]{2,1,0:T(1,128)}, u32[]{:S(2)}) copy-start(f32[4096,1,128]{2,1,0:T(1,128)} %param.6) | copy-start | bytes 6291460
  28.5 22.5 %copy-start.6 = (s32[2,8,128]{2,1,0:T(8,128)S(1)}, s32[2,8,128]{2,1,0:T(8,128)}, u32[]{:S(2)}) copy-start(s32[2,8,128]{2,1,0:T(8,128)} %get-tuple-element.10.starts) | copy-start | bytes 24580
  34.1 0.8 copy-start.2
  51.0 1.2 %copy-start.1 = (f32[2,8,128,128]{3,2,1,0:T(8,128)S(1)}, f32[2,8,128,128]{3,2,1,0:T(8,128)}, u32[]{:S(2)}) copy-start(f32[2,8,128,128]{3,2,1,0:T(8,128)} %send.1.arrived) | copy-start | bytes 3145732

commit v3 on v2

--- a/solution.py
+++ b/solution.py
@@ -264,49 +264,52 @@
                 total[at, :] += arrived[side, m, pl.ds(k * TILE, TILE), :]
 
 
-PIECE = SHARE // 2
-
-
-def reduce_kernel(total, out, up, down, final, spread, up_sem, down_sem, y_send, y_recv):
+CUT = SHARE // 2
+Z_ORDER = [4, 3, 5, 2, 6, 1, 7]
+
+
+def reduce_kernel(total, out, z_box, y_box, z_sum, y_sum, zy_box, yz_box, z_sem, y_sem, zy_sem, yz_sem):
     z, y, c, h, x = here()
     m = lax.axis_index("mdl")
-    above = ((((z + 1) % NZ) * NY + y) * 2 + c, m)
-    below = ((((z + NZ - 1) % NZ) * NY + y) * 2 + c, m)
-    others = [((z * NY + (y + d) % NY) * 2 + c, m) for d in range(1, NY)]
-    meet([above, below] + others)
-
-    rings = (
-        (up, up_sem, above, lambda s: (z + 2 * NZ - 1 - s) % NZ),
-        (down, down_sem, below, lambda s: (z + 1 + s) % NZ),
-    )
-    order = list(range(1, NY)) + [0]
-    flights, sends = {}, {}
-    for s in range(NZ):
-        for d in order:
-            for way, (box, sem, to, chunk) in enumerate(rings):
-                rows = pl.ds(way * PIECE, PIECE)
-                j = (y + d) % NY
-                if s:
-                    flights[s - 1, d, way].wait_recv()
-                if s == NZ - 1:
-                    final[d, rows, :] = box[s - 1, d] + total[z, j, c, rows, :]
-                    continue
-                src = total.at[chunk(0), j, c, rows, :]
-                if s:
-                    box[s - 1, d] += total[chunk(s), j, c, rows, :]
-                    src = box.at[s - 1, d]
-                flights[s, d, way] = remote(src, box.at[s, d], sem.at[0, s, d], sem.at[1, s, d], to)
-                flights[s, d, way].start()
-            if s == NZ - 1 and d:
-                sends[d] = remote(final.at[d], spread.at[d - 1], y_send.at[d - 1], y_recv.at[d - 1], others[d - 1])
-                sends[d].start()
-    acc = final[0]
-    for d in range(1, NY):
-        sends[d].wait()
-        acc = acc + spread[d - 1]
-    out[...] = acc
-    for f in flights.values():
-        f.wait_send()
+
+    def chip(dz, dy):
+        return ((((z + dz) % NZ) * NY + (y + dy) % NY) * 2 + c, m)
+
+    def send(src, dst, sem, i, to):
+        copy = remote(src, dst, sem.at[0, i], sem.at[1, i], to)
+        copy.start()
+        return copy
+
+    meet([chip(d, 0) for d in Z_ORDER] + [chip(0, d) for d in range(1, NY)])
+    low, high = pl.ds(0, CUT), pl.ds(CUT, SHARE - CUT)
+    along_z, along_y, then_y, then_z = {}, {}, {}, {}
+    for i, d in enumerate(Z_ORDER):
+        if i < NY - 1:
+            e = i + 1
+            along_y[e] = send(total.at[:, (y + e) % NY, c, high, :], y_box.at[e - 1], y_sem, e - 1, chip(0, e))
+        along_z[d] = send(total.at[(z + d) % NZ, :, c, low, :], z_box.at[d - 1], z_sem, d - 1, chip(d, 0))
+    for copy in along_y.values():
+        copy.wait_recv()
+    for d in Z_ORDER + [0]:
+        j = (z + d) % NZ
+        y_sum[d] = total[j, y, c, high, :] + sum(y_box[k, j] for k in range(NY - 1))
+        if d:
+            then_z[d] = send(y_sum.at[d], yz_box.at[d - 1], yz_sem, d - 1, chip(d, 0))
+    for copy in along_z.values():
+        copy.wait_recv()
+    for d in (2, 1, 3, 0):
+        j = (y + d) % NY
+        z_sum[d] = total[z, j, c, low, :] + sum(z_box[k, j] for k in range(NZ - 1))
+        if d:
+            then_y[d] = send(z_sum.at[d], zy_box.at[d - 1], zy_sem, d - 1, chip(0, d))
+    for copy in then_z.values():
+        copy.wait()
+    out[high, :] = y_sum[0] + sum(yz_box[k] for k in range(NZ - 1))
+    for copy in then_y.values():
+        copy.wait()
+    out[low, :] = z_sum[0] + sum(zy_box[k] for k in range(NY - 1))
+    for copy in list(along_z.values()) + list(along_y.values()):
+        copy.wait_send()
 
 
 def per_device(model, source, observed, owner_ids, offsets, lengths):
@@ -368,21 +371,22 @@
         compiler_params=pltpu.CompilerParams(vmem_limit_bytes=32 << 20),
         name="add",
     )(starts, arrived, block)
-    box = pltpu.VMEM((NZ - 1, NY, PIECE, 128), f32)
     gradient = pl.pallas_call(
         reduce_kernel,
         out_shape=jax.ShapeDtypeStruct((SHARE, 128), f32),
         in_specs=[VMEM],
         out_specs=VMEM,
         scratch_shapes=[
-            box,
-            box,
-            pltpu.VMEM((NY, SHARE, 128), f32),
-            pltpu.VMEM((NY - 1, SHARE, 128), f32),
-            dma((2, NZ - 1, NY)),
-            dma((2, NZ - 1, NY)),
-            dma((NY - 1,)),
-            dma((NY - 1,)),
+            pltpu.VMEM((NZ - 1, NY, CUT, 128), f32),
+            pltpu.VMEM((NY - 1, NZ, SHARE - CUT, 128), f32),
+            pltpu.VMEM((NY, CUT, 128), f32),
+            pltpu.VMEM((NZ, SHARE - CUT, 128), f32),
+            pltpu.VMEM((NY - 1, CUT, 128), f32),
+            pltpu.VMEM((NZ - 1, SHARE - CUT, 128), f32),
+            dma((2, NZ - 1)),
+            dma((2, NY - 1)),
+            dma((2, NY - 1)),
+            dma((2, NZ - 1)),
         ],
         compiler_params=pltpu.CompilerParams(
             collective_id=2, has_side_effects=True, vmem_limit_bytes=32 << 20

time: 92 us -> 84.3 us (0.916)
  the two profiles are of different devices: /device:TPU:24 before, /device:TPU:1 now
where the time goes in v3:
time: 84.3 us; the launch traced here: 83.9 us
  Pallas kernels  79 us (94%)
  local copies, waits for them, and re-layouts  4.85 us (6%)
    pallas_call x1, Pallas kernels, per_device(): pl.pallas_call(reduce_kernel, out_shape=jax.ShapeDtypeStruct((SHARE, 128)...  27.2 us
    pallas_call x1, Pallas kernels, per_device(): pl.pallas_call(fetch_kernel, out_shape=(jax.ShapeDtypeStruct((OWN, SLOT_R...  23.3 us
    pallas_call x1, Pallas kernels, per_device(): pl.pallas_call(send_kernel, out_shape=jax.ShapeDtypeStruct((2, OWN, SLOT_...  20.2 us
    pallas_call x1, Pallas kernels, per_device(): pl.pallas_call(solve_kernel, out_shape=jax.ShapeDtypeStruct((OWN * SLOT_R...  5.6 us
    unnamed x19, local copies, waits for them, and re-layouts  4.85 us

profile of v3, /device:TPU:1, one launch (start us, length us, event | category | flops | bytes accessed | tf_op | source)
XLA Modules:
  0.0 83.9 jit_solution(14779487045143803648)
XLA Ops:
  0.0 0.0 copy-start.7
  0.0 0.0 copy-start.3
  0.0 1.5 %tables.1 = (s32[16]{0:T(128)}, s32[8,128]{1,0:T(8,128)}) custom-call(s32[2,1,8]{2,1,0:T(1,128)} %bitcast.16, s32[2,8]{1,0:T(2,128)} %offset.1), custom_call_target="tpu_custom_call" | custom-call | tf_op jit(solution)/shard_map/tables/pallas_call | solution.py:319
  1.6 0.0 copy-start.8
  1.6 23.3 %fetch.1 = (f32[8,128,128]{2,1,0:T(8,128)}, s32[2,8,128]{2,1,0:T(8,128)}) custom-call(s32[8,128]{1,0:T(8,128)} %get-tuple-element.9.request, f32[4096,128]{1,0:T(8,128)} %bitcast.10), custom_call_target="tpu_custom_call" | custom-call | tf_op jit(solution)/shard_map/fetch/pallas_call | solution.py:327
  24.9 0.0 copy-done.7
  24.9 0.0 copy-done.3
  24.9 0.0 copy-done.8
  24.9 0.0 copy-start.4
  24.9 1.1 %copy-done.4 = f32[2,3,8,4096]{3,2,1,0:T(8,128)S(1)} copy-done((f32[2,3,8,4096]{3,2,1,0:T(8,128)S(1)}, f32[2,3,8,4096]{3,2,1,0:T(8,128)}, u32[]{:S(2)}) %copy-start.4) | copy-done | bytes 786456
  26.0 0.0 copy-start.5
  26.0 1.0 %copy-done.5 = f32[8,128,128]{2,1,0:T(8,128)S(1)} copy-done((f32[8,128,128]{2,1,0:T(8,128)S(1)}, f32[8,128,128]{2,1,0:T(8,128)}, u32[]{:S(2)}) %copy-start.5) | copy-done | bytes 524312
  27.1 0.0 copy-start
  27.1 0.0 copy-start.6
  27.1 5.6 %solve.1 = f32[1024,128]{1,0:T(8,128)S(1)} custom-call(s32[16]{0:T(128)S(1)} %copy-done.8, s32[2,8]{1,0:T(2,128)S(1)} %copy-done.7, f32[1024,128]{1,0:T(8,128)S(1)} %bitcast.14, f32[2,3,8,4096]{3,2,1,0:T(8,128)S(1)} %copy-done.3, f32[2,3,8,4096]{3,2,1,0:T(8,128)S(1)} %copy-done.4), custom_call_target="tpu_custom_call" | custom-call | tf_op jit(solution)/shard_map/solve/pallas_call | solution.py:340
  32.7 0.0 copy-start.2
  32.7 0.8 copy-done.2
  33.5 20.2 %send.1.arrived = f32[2,8,128,128]{3,2,1,0:T(8,128)} custom-call(f32[8,128,128]{2,1,0:T(8,128)} %bitcast.13), custom_call_target="tpu_custom_call" | custom-call | tf_op jit(solution)/shard_map/send/pallas_call | solution.py:357
  53.7 0.0 copy-done
  53.7 0.0 copy-done.6
  53.7 0.0 copy-start.1
  53.7 1.2 %copy-done.1 = f32[2,8,128,128]{3,2,1,0:T(8,128)S(1)} copy-done((f32[2,8,128,128]{3,2,1,0:T(8,128)S(1)}, f32[2,8,128,128]{3,2,1,0:T(8,128)}, u32[]{:S(2)}) %copy-start.1) | copy-done | bytes 1048600
  54.9 1.1 %add.1 = f32[4096,128]{1,0:T(8,128)S(1)} custom-call(s32[2,8,128]{2,1,0:T(8,128)S(1)} %copy-done.6, f32[2,8,128,128]{3,2,1,0:T(8,128)S(1)} %copy-done.1, f32[4096,128]{1,0:T(8,128)S(1)} %bitcast.11), custom_call_target="tpu_custom_call" | custom-call | tf_op jit(solution)/shard_map/add/pallas_call | solution.py:366
  56.1 27.2 %reduce.1 = f32[64,128]{1,0:T(8,128)S(1)} custom-call(f32[8,4,2,64,128]{4,3,2,1,0:T(8,128)S(1)} %bitcast.12), custom_call_target="tpu_custom_call" | custom-call | tf_op jit(solution)/shard_map/reduce/pallas_call | solution.py:374
  83.3 0.6 copy.10
Async XLA Ops:
  0.0 24.9 %copy-start.7 = (s32[2,8]{1,0:T(2,128)S(1)}, s32[2,8]{1,0:T(2,128)}, u32[]{:S(2)}) copy-start(s32[2,8]{1,0:T(2,128)} %lengths.1) | copy-start | bytes 196
  0.0 24.9 %copy-start.3 = (f32[2,3,8,4096]{3,2,1,0:T(8,128)S(1)}, f32[2,3,8,4096]{3,2,1,0:T(8,128)}, u32[]{:S(2)}) copy-start(f32[2,3,8,4096]{3,2,1,0:T(8,128)} %source.1) | copy-start | bytes 2359300
  1.6 23.3 %copy-start.8 = (s32[16]{0:T(128)S(1)}, s32[16]{0:T(128)}, u32[]{:S(2)}) copy-start(s32[16]{0:T(128)} %get-tuple-element.11.place) | copy-start | bytes 196
  24.9 1.1 %copy-start.4 = (f32[2,3,8,4096]{3,2,1,0:T(8,128)S(1)}, f32[2,3,8,4096]{3,2,1,0:T(8,128)}, u32[]{:S(2)}) copy-start(f32[2,3,8,4096]{3,2,1,0:T(8,128)} %observed.1) | copy-start | bytes 2359300
  26.0 1.0 %copy-start.5 = (f32[8,128,128]{2,1,0:T(8,128)S(1)}, f32[8,128,128]{2,1,0:T(8,128)}, u32[]{:S(2)}) copy-start(f32[8,128,128]{2,1,0:T(8,128)} %get-tuple-element.12) | copy-start | bytes 1572868
  27.1 26.6 %copy-start = (f32[4096,1,128]{2,1,0:T(1,128)S(1)}, f32[4096,1,128]{2,1,0:T(1,128)}, u32[]{:S(2)}) copy-start(f32[4096,1,128]{2,1,0:T(1,128)} %param.6) | copy-start | bytes 6291460
  27.1 26.6 %copy-start.6 = (s32[2,8,128]{2,1,0:T(8,128)S(1)}, s32[2,8,128]{2,1,0:T(8,128)}, u32[]{:S(2)}) copy-start(s32[2,8,128]{2,1,0:T(8,128)} %get-tuple-element.10.starts) | copy-start | bytes 24580
  32.7 0.8 copy-start.2
  53.7 1.2 %copy-start.1 = (f32[2,8,128,128]{3,2,1,0:T(8,128)S(1)}, f32[2,8,128,128]{3,2,1,0:T(8,128)}, u32[]{:S(2)}) copy-start(f32[2,8,128,128]{3,2,1,0:T(8,128)} %send.1.arrived) | copy-start | bytes 3145732

commit v4 on v3

--- a/solution.py
+++ b/solution.py
@@ -25,6 +25,7 @@
 SMEM = pl.BlockSpec(memory_space=pltpu.SMEM)
 VMEM = pl.BlockSpec(memory_space=pltpu.VMEM)
 FAR_FIRST = [(1, 2), (1, 1), (1, 3), (1, 0), (0, 2), (0, 1), (0, 3)]
+Z_ORDER = [4, 3, 5, 2, 6, 1, 7]
 
 
 def here():
@@ -32,11 +33,11 @@
     return g // (2 * NY), (g // 2) % NY, g % 2, m // NX, m % NX
 
 
-def partner(dh, dx):
+def partner(dh, dx, dz=0):
     z, y, c, h, x = here()
     y = NY - 1 - y if dh % 2 else y
     m = ((h + dh) % 2) * NX + (x + dx) % NX
-    return ((z * NY + y) * 2 + c, m), m
+    return ((((z + dz) % NZ) * NY + y) * 2 + c, m), m
 
 
 def other_core():
@@ -70,40 +71,51 @@
         request[o, k] = offset[t // LZ, t % LZ]
 
 
-def fetch_kernel(request, block, values, starts, outbox, ask_send, ask_recv, row_send, row_recv, core_sem):
+def fetch_kernel(
+    request, block, values, starts, outbox, ask_send, ask_recv, row_send, row_recv, core_sem, z_send, z_recv
+):
     me = lax.axis_index("mdl")
-    meet([partner(*d)[0] for d in FAR_FIRST] + [other_core()])
+    z = here()[0]
+    z_ids = {d: partner(0, 0, d)[0] for d in Z_ORDER}
+    meet([partner(*d)[0] for d in FAR_FIRST] + [other_core()] + list(z_ids.values()))
     asks, answers = {}, {}
     for dh, dx in FAR_FIRST:
         to, m = partner(dh, dx)
         k = dh * NX + dx
-        asks[dh, dx] = remote(request.at[m], starts.at[0, me], ask_send.at[k], ask_recv.at[k], to)
+        asks[dh, dx] = remote(request.at[m], starts.at[z, 0, me], ask_send.at[k], ask_recv.at[k], to)
         asks[dh, dx].start()
     for k in range(CAP):
-        starts[0, me, k] = request[me, k]
+        starts[z, 0, me, k] = request[me, k]
     for dh, dx in FAR_FIRST:
         back = (-dh % 2, -dx % NX)
         asks[back].wait_recv()
         to, m = partner(dh, dx)
         k = dh * NX + dx
         for i in range(CAP):
-            outbox[k, pl.ds(i * TILE, TILE), :] = block[pl.ds(starts[0, m, i], TILE), :]
+            outbox[k, pl.ds(i * TILE, TILE), :] = block[pl.ds(starts[z, 0, m, i], TILE), :]
         answers[dh, dx] = remote(outbox.at[k], values.at[me], row_send.at[k], row_recv.at[k], to)
         answers[dh, dx].start()
-    pass_on = remote(starts.at[0], starts.at[1], core_sem.at[0], core_sem.at[1], other_core())
+    pass_on = remote(starts.at[z, 0], starts.at[z, 1], core_sem.at[0], core_sem.at[1], other_core())
     pass_on.start()
     for k in range(CAP):
-        values[me, pl.ds(k * TILE, TILE), :] = block[pl.ds(starts[0, me, k], TILE), :]
+        values[me, pl.ds(k * TILE, TILE), :] = block[pl.ds(starts[z, 0, me, k], TILE), :]
+    pass_on.wait()
+    tables = [remote(starts.at[z], starts.at[z], z_send.at[d], z_recv.at[d], z_ids[d]) for d in Z_ORDER]
+    for copy in tables:
+        copy.start()
     for d in FAR_FIRST:
         asks[d].wait_send()
         answers[d].wait()
-    pass_on.wait()
+    for copy in tables:
+        copy.wait()
 
 
 BATCH = 4
 
 
-def solve_kernel(place, lengths, values, source, observed, out, cond, weight, first, second, third, rhs, part):
+def solve_kernel(
+    place, lengths, values, source, observed, out, cond, weight, first, second, third, rhs, part, by_row
+):
     lane = lax.broadcasted_iota(jnp.int32, (8, 128), 1)
     layer = lax.broadcasted_iota(jnp.int32, (8, 128), 0)
     low = lane < 64
@@ -213,103 +225,104 @@
                 at = pl.ds((k + d) * 8, 8)
                 part[s, at, :] = -cond[s, at, :] * v
 
-    out[...] = jnp.zeros_like(out)
+    by_row[...] = jnp.zeros_like(by_row)
     for t in range(TILES):
         s, z = t // LZ, t % LZ
         got = part[s, pl.ds(z, TILE, stride=8), :]
-        out[pl.ds(pl.multiple_of(place[t] * TILE, TILE), TILE), :] = jnp.where(row < lengths[s, z], got, 0.0)
-
-
-def send_kernel(slots, arrived, send, recv, core_send, core_recv, own_sem):
+        by_row[pl.ds(pl.multiple_of(place[t] * TILE, TILE), TILE), :] = jnp.where(row < lengths[s, z], got, 0.0)
+    for o in range(OWN):
+        cells = by_row[pl.ds(o * SLOT_ROWS, SLOT_ROWS), :].T.reshape(NZ, 2, 8, 128)
+        for k in range(2):
+            out[k, o] = cells[:, k]
+
+
+SPREAD = [(dh, dx, dz) for dz in Z_ORDER + [0] for dh, dx in FAR_FIRST + [(0, 0)] if (dh, dx, dz) != (0, 0, 0)]
+
+
+def send_kernel(slots, arrived, pair, send, recv, core_send, core_recv, own_sem):
     me = lax.axis_index("mdl")
-    meet([partner(*d)[0] for d in FAR_FIRST] + [other_core()])
-    copies, forwards = {}, []
-    for dh, dx in FAR_FIRST:
-        to, m = partner(dh, dx)
-        k = dh * NX + dx
-        copies[dh, dx] = remote(slots.at[m], arrived.at[0, me], send.at[k], recv.at[k], to)
-        copies[dh, dx].start()
-    own = pltpu.make_async_copy(slots.at[me], arrived.at[0, me], own_sem)
+    z, y, c, h, x = here()
+    meet([partner(*d)[0] for d in SPREAD] + [other_core()])
+    swap = remote(slots.at[1 - c], pair.at[1], core_send, core_recv, other_core())
+    swap.start()
+    keep = pltpu.make_async_copy(slots.at[c], pair.at[0], own_sem)
+    keep.start()
+    keep.wait()
+    swap.wait()
+    copies = []
+    for dh, dx, dz in SPREAD:
+        to, m = partner(dh, dx, dz)
+        k = (dh * NX + dx) * NZ + dz
+        copies.append(remote(pair.at[:, m, (z + dz) % NZ], arrived.at[k], send, recv, to))
+        copies[-1].start()
+    own = pltpu.make_async_copy(pair.at[:, me, z], arrived.at[0], own_sem)
     own.start()
-    forwards.append(remote(slots.at[me], arrived.at[1, me], core_send.at[0], core_recv.at[0], other_core()))
-    forwards[0].start()
-    for dh, dx in FAR_FIRST[::-1]:
-        _, m = partner(dh, dx)
-        back = (-dh % 2, -dx % NX)
-        copies[back].wait_recv()
-        k = dh * NX + dx
-        forwards.append(
-            remote(arrived.at[0, m], arrived.at[1, m], core_send.at[k], core_recv.at[k], other_core())
-        )
-        forwards[-1].start()
     own.wait()
-    for d in FAR_FIRST:
-        copies[d].wait_send()
-    for f in forwards:
-        f.wait()
-
-
-def add_kernel(starts, arrived, block, total):
-    total[...] = jnp.zeros_like(total)
+    others = pl.ds(1, OWN * NZ - 1)
+    pltpu.make_async_copy(arrived.at[others], arrived.at[others], recv).wait()
+    pltpu.make_async_copy(arrived.at[others], arrived.at[others], send).wait()
+
+
+PARTS = 2 * CAP
+
+
+def add_kernel(starts, arrived, block, total, smooth, sums):
+    z, y, c, h, x = here()
     at = pl.ds(pl.multiple_of(lax.axis_index("grp") * SHARE, SHARE), SHARE)
     mine = block[at, :]
     lane = lax.broadcasted_iota(jnp.int32, (SHARE, 128), 1)
     left = jnp.where(lane == 0, mine, pltpu.roll(mine, 1, 1))
     right = jnp.where(lane == 127, mine, pltpu.roll(mine, 127, 1))
-    total[at, :] = BETA * (2.0 * mine - left - right)
-    for side in range(2):
-        for m in range(OWN):
-            for k in range(CAP):
-                at = pl.ds(starts[side, m, k], TILE)
-                total[at, :] += arrived[side, m, pl.ds(k * TILE, TILE), :]
-
-
-CUT = SHARE // 2
-Z_ORDER = [4, 3, 5, 2, 6, 1, 7]
-
-
-def reduce_kernel(total, out, z_box, y_box, z_sum, y_sum, zy_box, yz_box, z_sem, y_sem, zy_sem, yz_sem):
+    smooth[...] = BETA * (2.0 * mine - left - right)
+
+    sums[...] = jnp.zeros_like(sums)
+    lane = lax.broadcasted_iota(jnp.int32, (8, 128), 1)
+
+    def one(k, carry):
+        dz, dx, dh = k % NZ, (k // NZ) % NX, k // (NZ * NX)
+        zs = (z + NZ - dz) % NZ
+        ms = ((h + 2 - dh) % 2) * NX + (x + NX - dx) % NX
+        for side in range(2):
+            v = arrived[k, side]
+            for i in range(CAP):
+                start = starts[zs, side, ms, i]
+                a, r = start // 128, start % 128
+                moved = pltpu.roll(v, (r + 128 - i * TILE) % 128, 1)
+                moved = jnp.where(((lane - r) & 127) < TILE, moved, 0.0)
+                p = side * CAP + i
+                sums[p, a] += jnp.where(lane >= r, moved, 0.0)
+                sums[p, a + 1] += jnp.where(lane >= r, 0.0, moved)
+        return carry
+
+    lax.fori_loop(0, OWN * NZ, one, 0, unroll=2)
+    total[...] = sum(sums[p, pl.ds(0, TILE)] for p in range(PARTS))
+
+
+PLANE = [(dz, dy) for dz in Z_ORDER + [0] for dy in (2, 1, 3, 0) if (dz, dy) != (0, 0)]
+
+
+def reduce_kernel(total, smooth, out, box, cells, turned, send, recv, core_send, core_recv):
     z, y, c, h, x = here()
     m = lax.axis_index("mdl")
 
     def chip(dz, dy):
         return ((((z + dz) % NZ) * NY + (y + dy) % NY) * 2 + c, m)
 
-    def send(src, dst, sem, i, to):
-        copy = remote(src, dst, sem.at[0, i], sem.at[1, i], to)
-        copy.start()
-        return copy
-
-    meet([chip(d, 0) for d in Z_ORDER] + [chip(0, d) for d in range(1, NY)])
-    low, high = pl.ds(0, CUT), pl.ds(CUT, SHARE - CUT)
-    along_z, along_y, then_y, then_z = {}, {}, {}, {}
-    for i, d in enumerate(Z_ORDER):
-        if i < NY - 1:
-            e = i + 1
-            along_y[e] = send(total.at[:, (y + e) % NY, c, high, :], y_box.at[e - 1], y_sem, e - 1, chip(0, e))
-        along_z[d] = send(total.at[(z + d) % NZ, :, c, low, :], z_box.at[d - 1], z_sem, d - 1, chip(d, 0))
-    for copy in along_y.values():
-        copy.wait_recv()
-    for d in Z_ORDER + [0]:
-        j = (z + d) % NZ
-        y_sum[d] = total[j, y, c, high, :] + sum(y_box[k, j] for k in range(NY - 1))
-        if d:
-            then_z[d] = send(y_sum.at[d], yz_box.at[d - 1], yz_sem, d - 1, chip(d, 0))
-    for copy in along_z.values():
-        copy.wait_recv()
-    for d in (2, 1, 3, 0):
-        j = (y + d) % NY
-        z_sum[d] = total[z, j, c, low, :] + sum(z_box[k, j] for k in range(NZ - 1))
-        if d:
-            then_y[d] = send(z_sum.at[d], zy_box.at[d - 1], zy_sem, d - 1, chip(0, d))
-    for copy in then_z.values():
-        copy.wait()
-    out[high, :] = y_sum[0] + sum(yz_box[k] for k in range(NZ - 1))
-    for copy in then_y.values():
-        copy.wait()
-    out[low, :] = z_sum[0] + sum(zy_box[k] for k in range(NY - 1))
-    for copy in list(along_z.values()) + list(along_y.values()):
-        copy.wait_send()
+    meet([chip(*d) for d in PLANE] + [other_core()])
+    for dz, dy in PLANE:
+        src = total.at[((z + dz) % NZ) * NY + (y + dy) % NY]
+        remote(src, box.at[dz * NY + dy], send, recv, chip(dz, dy)).start()
+    others = pl.ds(1, NZ * NY - 1)
+    pltpu.make_async_copy(box.at[others], box.at[others], recv).wait()
+    box[0] = total[z * NY + y]
+    for dz in range(NZ):
+        cells[(z + NZ - dz) % NZ, c] = sum(box[dz * NY + dy] for dy in range(NY))
+    swap = remote(cells.at[:, c], cells.at[:, c], core_send, core_recv, other_core())
+    swap.start()
+    swap.wait()
+    turned[...] = cells[...].reshape(128, 128).T.reshape(2, SHARE, 128)
+    out[...] = turned[c] + smooth[...]
+    pltpu.make_async_copy(box.at[others], box.at[others], send).wait()
 
 
 def per_device(model, source, observed, owner_ids, offsets, lengths):
@@ -328,18 +341,20 @@
         fetch_kernel,
         out_shape=(
             jax.ShapeDtypeStruct((OWN, SLOT_ROWS, 128), f32),
-            jax.ShapeDtypeStruct((2, OWN, 128), i32),
+            jax.ShapeDtypeStruct((NZ, 2, OWN, 128), i32),
         ),
         in_specs=[SMEM, VMEM],
         out_specs=(VMEM, SMEM),
-        scratch_shapes=[pltpu.VMEM((OWN, SLOT_ROWS, 128), f32)] + [dma((OWN,))] * 4 + [dma((2,))],
+        scratch_shapes=[pltpu.VMEM((OWN, SLOT_ROWS, 128), f32)]
+        + [dma((OWN,))] * 4
+        + [dma((2,)), dma((NZ,)), dma((NZ,))],
         compiler_params=pltpu.CompilerParams(collective_id=0, has_side_effects=True),
         name="fetch",
     )(request, block)
     fields = pltpu.VMEM((S_DEV, 3, TILE + 1, 8, 128), f32)
     slots = pl.pallas_call(
         solve_kernel,
-        out_shape=jax.ShapeDtypeStruct((OWN * SLOT_ROWS, 128), f32),
+        out_shape=jax.ShapeDtypeStruct((2, OWN, NZ, 8, 128), f32),
         in_specs=[SMEM, SMEM, VMEM, VMEM, VMEM],
         out_specs=VMEM,
         scratch_shapes=[
@@ -350,49 +365,48 @@
             fields,
             pltpu.VMEM((S_DEV, 3, TILE, 8, 128), f32),
             pltpu.VMEM((S_DEV, TILE * 8, 128), f32),
+            pltpu.VMEM((OWN * SLOT_ROWS, 128), f32),
         ],
         compiler_params=pltpu.CompilerParams(vmem_limit_bytes=32 << 20),
         name="solve",
     )(place, lengths, values.reshape(OWN * SLOT_ROWS, 128), source, observed)
     arrived = pl.pallas_call(
         send_kernel,
-        out_shape=jax.ShapeDtypeStruct((2, OWN, SLOT_ROWS, 128), f32),
+        out_shape=jax.ShapeDtypeStruct((OWN * NZ, 2, 8, 128), f32),
         in_specs=[VMEM],
         out_specs=VMEM,
-        scratch_shapes=[dma((OWN,))] * 4 + [dma],
+        scratch_shapes=[pltpu.VMEM((2, OWN, NZ, 8, 128), f32)] + [dma] * 5,
         compiler_params=pltpu.CompilerParams(collective_id=1, has_side_effects=True),
         name="send",
-    )(slots.reshape(OWN, SLOT_ROWS, 128))
-    total = pl.pallas_call(
+    )(slots)
+    total, smooth = pl.pallas_call(
         add_kernel,
-        out_shape=jax.ShapeDtypeStruct((ROWS, 128), f32),
+        out_shape=(
+            jax.ShapeDtypeStruct((NZ * NY, 8, 128), f32),
+            jax.ShapeDtypeStruct((SHARE, 128), f32),
+        ),
         in_specs=[SMEM, VMEM, VMEM],
-        out_specs=VMEM,
+        out_specs=(VMEM, VMEM),
+        scratch_shapes=[pltpu.VMEM((PARTS, TILE + 1, 8, 128), f32)],
         compiler_params=pltpu.CompilerParams(vmem_limit_bytes=32 << 20),
         name="add",
     )(starts, arrived, block)
     gradient = pl.pallas_call(
         reduce_kernel,
         out_shape=jax.ShapeDtypeStruct((SHARE, 128), f32),
-        in_specs=[VMEM],
+        in_specs=[VMEM, VMEM],
         out_specs=VMEM,
         scratch_shapes=[
-            pltpu.VMEM((NZ - 1, NY, CUT, 128), f32),
-            pltpu.VMEM((NY - 1, NZ, SHARE - CUT, 128), f32),
-            pltpu.VMEM((NY, CUT, 128), f32),
-            pltpu.VMEM((NZ, SHARE - CUT, 128), f32),
-            pltpu.VMEM((NY - 1, CUT, 128), f32),
-            pltpu.VMEM((NZ - 1, SHARE - CUT, 128), f32),
-            dma((2, NZ - 1)),
-            dma((2, NY - 1)),
-            dma((2, NY - 1)),
-            dma((2, NZ - 1)),
-        ],
+            pltpu.VMEM((NZ * NY, 8, 128), f32),
+            pltpu.VMEM((NZ, 2, 8, 128), f32),
+            pltpu.VMEM((2, SHARE, 128), f32),
+        ]
+        + [dma] * 4,
         compiler_params=pltpu.CompilerParams(
             collective_id=2, has_side_effects=True, vmem_limit_bytes=32 << 20
         ),
         name="reduce",
-    )(total.reshape(NZ, NY, 2, SHARE, 128))
+    )(total, smooth)
     return gradient[:, None, :]
 
 

time: 84.3 us -> 94.6 us (1.12)
  Pallas kernels: 79 us -> 89.3 us
    pallas_call x3, Pallas kernels: 26.9 us -> 43.7 us  [the longest x1 28.8 us: per_device(): pl.pallas_call(send_kernel, out_shape=jax.ShapeDtypeStruct((OWN * NZ, 2,...]
    pallas_call x1, Pallas kernels: 27.2 us -> 13.7 us  [per_device(): pl.pallas_call(reduce_kernel, out_shape=jax.ShapeDtypeStruct((SHARE, 128)...]
    pallas_call x1, Pallas kernels: 23.3 us -> 30.3 us  [per_device(): pl.pallas_call(fetch_kernel, out_shape=(jax.ShapeDtypeStruct((OWN, SLOT_R...]
where the time goes in v4:
time: 94.6 us; the launch traced here: 94.2 us
  Pallas kernels  89.3 us (94%)
  local copies, waits for them, and re-layouts  4.76 us (5%)
    pallas_call x1, Pallas kernels, per_device(): pl.pallas_call(fetch_kernel, out_shape=(jax.ShapeDtypeStruct((OWN, SLOT_R...  30.3 us
    pallas_call x1, Pallas kernels, per_device(): pl.pallas_call(send_kernel, out_shape=jax.ShapeDtypeStruct((OWN * NZ, 2,...  28.8 us
    pallas_call x1, Pallas kernels, per_device(): pl.pallas_call(reduce_kernel, out_shape=jax.ShapeDtypeStruct((SHARE, 128)...  13.7 us
    pallas_call x1, Pallas kernels, per_device(): pl.pallas_call(add_kernel, out_shape=(jax.ShapeDtypeStruct((NZ * NY, 8, 1...  9.15 us
    pallas_call x1, Pallas kernels, per_device(): pl.pallas_call(solve_kernel, out_shape=jax.ShapeDtypeStruct((2, OWN, NZ,...  5.8 us
    unnamed x19, local copies, waits for them, and re-layouts  4.76 us

profile of v4, /device:TPU:1, one launch (start us, length us, event | category | flops | bytes accessed | tf_op | source)
XLA Modules:
  0.0 94.2 jit_solution(797469105910971095)
XLA Ops:
  0.0 0.0 copy-start.7
  0.0 0.0 copy-start.3
  0.0 1.5 %tables.1 = (s32[16]{0:T(128)}, s32[8,128]{1,0:T(8,128)}) custom-call(s32[2,1,8]{2,1,0:T(1,128)} %bitcast.12, s32[2,8]{1,0:T(2,128)} %offset.1), custom_call_target="tpu_custom_call" | custom-call | tf_op jit(solution)/shard_map/tables/pallas_call | solution.py:332
  1.6 0.0 copy-start.8
  1.6 30.3 %fetch.1 = (f32[8,128,128]{2,1,0:T(8,128)}, s32[8,2,8,128]{3,2,1,0:T(8,128)}) custom-call(s32[8,128]{1,0:T(8,128)} %get-tuple-element.11.request, f32[4096,128]{1,0:T(8,128)} %bitcast.8), custom_call_target="tpu_custom_call" | custom-call | tf_op jit(solution)/shard_map/fetch/pallas_call | solution.py:340
  31.9 0.0 copy-start
  31.9 0.0 copy-done.7
  31.9 0.0 copy-done.3
  32.0 0.0 copy-done.8
  32.0 0.0 copy-start.4
  32.0 1.3 %copy-done.4 = f32[2,3,8,4096]{3,2,1,0:T(8,128)S(1)} copy-done((f32[2,3,8,4096]{3,2,1,0:T(8,128)S(1)}, f32[2,3,8,4096]{3,2,1,0:T(8,128)}, u32[]{:S(2)}) %copy-start.4) | copy-done | bytes 786456
  33.2 0.0 copy-start.5
  33.2 1.0 %copy-done.5 = f32[8,128,128]{2,1,0:T(8,128)S(1)} copy-done((f32[8,128,128]{2,1,0:T(8,128)S(1)}, f32[8,128,128]{2,1,0:T(8,128)}, u32[]{:S(2)}) %copy-start.5) | copy-done | bytes 524312
  34.3 0.0 copy-start.6
  34.3 5.8 %solve.1.slots = f32[2,8,8,8,128]{4,3,2,1,0:T(8,128)S(1)} custom-call(s32[16]{0:T(128)S(1)} %copy-done.8, s32[2,8]{1,0:T(2,128)S(1)} %copy-done.7, f32[1024,128]{1,0:T(8,128)S(1)} %bitcast.10, f32[2,3,8,4096]{3,2,1,0:T(8,128)S(1)} %copy-done.3, f32[2,3,8,4096]{3,2,1,0:T(8,128)S(1)} %copy-done.4), custom_call_target="tpu_custom_call" | custom-call | tf_op jit(solution)/shard_map/solve/pallas_call | solution.py:355
  40.1 0.0 copy-start.2
  40.1 0.8 copy-done.2
  40.9 28.8 %send.1.arrived = f32[64,2,8,128]{3,2,1,0:T(8,128)} custom-call(f32[2,8,8,8,128]{4,3,2,1,0:T(8,128)} %copy-done.2), custom_call_target="tpu_custom_call" | custom-call | tf_op jit(solution)/shard_map/send/pallas_call | solution.py:373
  69.7 0.0 copy-done
  69.7 0.0 copy-done.6
  69.7 0.0 copy-start.1
  69.7 1.0 %copy-done.1 = f32[64,2,8,128]{3,2,1,0:T(8,128)S(1)} copy-done((f32[64,2,8,128]{3,2,1,0:T(8,128)S(1)}, f32[64,2,8,128]{3,2,1,0:T(8,128)}, u32[]{:S(2)}) %copy-start.1) | copy-done | bytes 524312
  70.7 9.2 %add.1 = (f32[32,8,128]{2,1,0:T(8,128)S(1)}, f32[64,128]{1,0:T(8,128)S(1)}) custom-call(s32[8,2,8,128]{3,2,1,0:T(8,128)S(1)} %copy-done.6, f32[64,2,8,128]{3,2,1,0:T(8,128)S(1)} %copy-done.1, f32[4096,128]{1,0:T(8,128)S(1)} %bitcast.9), custom_call_target="tpu_custom_call" | custom-call | tf_op jit(solution)/shard_map/add/pallas_call | solution.py:382
  79.9 13.7 %reduce.1 = f32[64,128]{1,0:T(8,128)S(1)} custom-call(f32[32,8,128]{2,1,0:T(8,128)S(1)} %get-tuple-element.15.total, f32[64,128]{1,0:T(8,128)S(1)} %get-tuple-element.16.smooth), custom_call_target="tpu_custom_call" | custom-call | tf_op jit(solution)/shard_map/reduce/pallas_call | solution.py:394
  93.6 0.6 copy.10
Async XLA Ops:
  0.0 31.9 %copy-start.7 = (s32[2,8]{1,0:T(2,128)S(1)}, s32[2,8]{1,0:T(2,128)}, u32[]{:S(2)}) copy-start(s32[2,8]{1,0:T(2,128)} %lengths.1) | copy-start | bytes 196
  0.0 31.9 %copy-start.3 = (f32[2,3,8,4096]{3,2,1,0:T(8,128)S(1)}, f32[2,3,8,4096]{3,2,1,0:T(8,128)}, u32[]{:S(2)}) copy-start(f32[2,3,8,4096]{3,2,1,0:T(8,128)} %source.1) | copy-start | bytes 2359300
  1.6 30.4 %copy-start.8 = (s32[16]{0:T(128)S(1)}, s32[16]{0:T(128)}, u32[]{:S(2)}) copy-start(s32[16]{0:T(128)} %get-tuple-element.13.place) | copy-start | bytes 196
  31.9 37.8 %copy-start = (f32[4096,1,128]{2,1,0:T(1,128)S(1)}, f32[4096,1,128]{2,1,0:T(1,128)}, u32[]{:S(2)}) copy-start(f32[4096,1,128]{2,1,0:T(1,128)} %param.6) | copy-start | bytes 6291460
  32.0 1.3 %copy-start.4 = (f32[2,3,8,4096]{3,2,1,0:T(8,128)S(1)}, f32[2,3,8,4096]{3,2,1,0:T(8,128)}, u32[]{:S(2)}) copy-start(f32[2,3,8,4096]{3,2,1,0:T(8,128)} %observed.1) | copy-start | bytes 2359300
  33.2 1.0 %copy-start.5 = (f32[8,128,128]{2,1,0:T(8,128)S(1)}, f32[8,128,128]{2,1,0:T(8,128)}, u32[]{:S(2)}) copy-start(f32[8,128,128]{2,1,0:T(8,128)} %get-tuple-element.14) | copy-start | bytes 1572868
  34.3 35.4 %copy-start.6 = (s32[8,2,8,128]{3,2,1,0:T(8,128)S(1)}, s32[8,2,8,128]{3,2,1,0:T(8,128)}, u32[]{:S(2)}) copy-start(s32[8,2,8,128]{3,2,1,0:T(8,128)} %get-tuple-element.12.starts) | copy-start | bytes 196612
  40.1 0.8 copy-start.2
  69.7 1.0 %copy-start.1 = (f32[64,2,8,128]{3,2,1,0:T(8,128)S(1)}, f32[64,2,8,128]{3,2,1,0:T(8,128)}, u32[]{:S(2)}) copy-start(f32[64,2,8,128]{3,2,1,0:T(8,128)} %send.1.arrived) | copy-start | bytes 1572868

commit v5 on v3

--- a/solution.py
+++ b/solution.py
@@ -24,6 +24,7 @@
 MESH = pl.DeviceIdType.MESH
 SMEM = pl.BlockSpec(memory_space=pltpu.SMEM)
 VMEM = pl.BlockSpec(memory_space=pltpu.VMEM)
+HBM = pl.BlockSpec(memory_space=pl.ANY)
 FAR_FIRST = [(1, 2), (1, 1), (1, 3), (1, 0), (0, 2), (0, 1), (0, 3)]
 
 
@@ -57,53 +58,25 @@
     )
 
 
-def tables_kernel(owner, offset, place, request, counts):
+def tables_kernel(owner, offset, place, holds, request, counts):
     for o in range(OWN):
         counts[o] = 0
         for k in range(CAP):
             request[o, k] = 0
+            holds[o * CAP + k] = TILES * TILE
     for t in range(TILES):
         o = owner[t // LZ, 0, t % LZ]
         k = counts[o]
         counts[o] = k + 1
-        place[t] = o * CAP + k
+        place[t] = (o * CAP + k) * TILE
+        holds[o * CAP + k] = t * TILE
         request[o, k] = offset[t // LZ, t % LZ]
 
 
-def fetch_kernel(request, block, values, starts, outbox, ask_send, ask_recv, row_send, row_recv, core_sem):
-    me = lax.axis_index("mdl")
-    meet([partner(*d)[0] for d in FAR_FIRST] + [other_core()])
-    asks, answers = {}, {}
-    for dh, dx in FAR_FIRST:
-        to, m = partner(dh, dx)
-        k = dh * NX + dx
-        asks[dh, dx] = remote(request.at[m], starts.at[0, me], ask_send.at[k], ask_recv.at[k], to)
-        asks[dh, dx].start()
-    for k in range(CAP):
-        starts[0, me, k] = request[me, k]
-    for dh, dx in FAR_FIRST:
-        back = (-dh % 2, -dx % NX)
-        asks[back].wait_recv()
-        to, m = partner(dh, dx)
-        k = dh * NX + dx
-        for i in range(CAP):
-            outbox[k, pl.ds(i * TILE, TILE), :] = block[pl.ds(starts[0, m, i], TILE), :]
-        answers[dh, dx] = remote(outbox.at[k], values.at[me], row_send.at[k], row_recv.at[k], to)
-        answers[dh, dx].start()
-    pass_on = remote(starts.at[0], starts.at[1], core_sem.at[0], core_sem.at[1], other_core())
-    pass_on.start()
-    for k in range(CAP):
-        values[me, pl.ds(k * TILE, TILE), :] = block[pl.ds(starts[0, me, k], TILE), :]
-    for d in FAR_FIRST:
-        asks[d].wait_send()
-        answers[d].wait()
-    pass_on.wait()
-
-
 BATCH = 4
 
 
-def solve_kernel(place, lengths, values, source, observed, out, cond, weight, first, second, third, rhs, part):
+def solve(place, lengths, values, source, observed, by_layer, cond, weight, first, second, third, rhs, part):
     lane = lax.broadcasted_iota(jnp.int32, (8, 128), 1)
     layer = lax.broadcasted_iota(jnp.int32, (8, 128), 0)
     low = lane < 64
@@ -125,7 +98,7 @@
 
     for t in range(TILES):
         s, z = t // LZ, t % LZ
-        got = values[pl.ds(pl.multiple_of(place[t] * TILE, TILE), TILE), :]
+        got = values[pl.ds(place[t], TILE), :]
         cond[s, pl.ds(z, TILE, stride=8), :] = jnp.where(row < lengths[s, z], jnp.exp(got), AIR)
 
     def split(a, b):
@@ -213,23 +186,92 @@
                 at = pl.ds((k + d) * 8, 8)
                 part[s, at, :] = -cond[s, at, :] * v
 
-    out[...] = jnp.zeros_like(out)
     for t in range(TILES):
         s, z = t // LZ, t % LZ
         got = part[s, pl.ds(z, TILE, stride=8), :]
-        out[pl.ds(pl.multiple_of(place[t] * TILE, TILE), TILE), :] = jnp.where(row < lengths[s, z], got, 0.0)
-
-
-def send_kernel(slots, arrived, send, recv, core_send, core_recv, own_sem):
+        by_layer[pl.ds(t * TILE, TILE), :] = jnp.where(row < lengths[s, z], got, 0.0)
+    by_layer[pl.ds(TILES * TILE, TILE), :] = jnp.zeros((TILE, 128), jnp.float32)
+
+
+def front_kernel(
+    place,
+    holds,
+    request,
+    lengths,
+    block_hbm,
+    source_hbm,
+    observed_hbm,
+    arrived,
+    starts,
+    block,
+    source,
+    observed,
+    values,
+    outbox,
+    slots,
+    by_layer,
+    *rest,
+):
+    fields, (load_sem, ask_send, ask_recv, row_send, row_recv, send, recv, core_send, core_recv, core_sem) = (
+        rest[:7],
+        rest[7:],
+    )
     me = lax.axis_index("mdl")
-    meet([partner(*d)[0] for d in FAR_FIRST] + [other_core()])
+    barrier = pltpu.get_barrier_semaphore()
+    greeted = [partner(*d)[0] for d in FAR_FIRST] + [other_core()]
+    for i in greeted:
+        pl.semaphore_signal(barrier, inc=1, device_id=i, device_id_type=MESH)
+    pairs = ((block_hbm, block), (source_hbm, source), (observed_hbm, observed))
+    loads = [pltpu.make_async_copy(a, b, load_sem.at[i]) for i, (a, b) in enumerate(pairs)]
+    for copy in loads:
+        copy.start()
+    pl.semaphore_wait(barrier, len(greeted))
+
+    asks, answers = {}, {}
+    for dh, dx in FAR_FIRST:
+        to, m = partner(dh, dx)
+        k = dh * NX + dx
+        asks[dh, dx] = remote(request.at[m], starts.at[0, me], ask_send.at[k], ask_recv.at[k], to)
+        asks[dh, dx].start()
+    for k in range(CAP):
+        starts[0, me, k] = request[me, k]
+    loads[0].wait()
+    for dh, dx in FAR_FIRST:
+        back = (-dh % 2, -dx % NX)
+        asks[back].wait_recv()
+        to, m = partner(dh, dx)
+        k = dh * NX + dx
+        for i in range(CAP):
+            outbox[k, pl.ds(i * TILE, TILE), :] = block[pl.ds(starts[0, m, i], TILE), :]
+        answers[dh, dx] = remote(
+            outbox.at[k], values.at[pl.ds(me * SLOT_ROWS, SLOT_ROWS)], row_send.at[k], row_recv.at[k], to
+        )
+        answers[dh, dx].start()
+    pass_on = remote(starts.at[0], starts.at[1], core_sem.at[0], core_sem.at[1], other_core())
+    pass_on.start()
+    for k in range(CAP):
+        at = pl.ds(me * SLOT_ROWS + k * TILE, TILE)
+        values[at, :] = block[pl.ds(starts[0, me, k], TILE), :]
+    for copy in loads[1:]:
+        copy.wait()
+    for d in FAR_FIRST:
+        answers[d].wait_recv()
+
+    solve(place, lengths, values, source, observed, by_layer, *fields)
+
+    def fill(m):
+        for k in range(CAP):
+            slots[m, pl.ds(k * TILE, TILE), :] = by_layer[pl.ds(holds[m * CAP + k], TILE), :]
+
     copies, forwards = {}, []
     for dh, dx in FAR_FIRST:
         to, m = partner(dh, dx)
         k = dh * NX + dx
+        fill(m)
         copies[dh, dx] = remote(slots.at[m], arrived.at[0, me], send.at[k], recv.at[k], to)
         copies[dh, dx].start()
-    own = pltpu.make_async_copy(slots.at[me], arrived.at[0, me], own_sem)
+    fill(me)
+    own = pltpu.make_async_copy(slots.at[me], arrived.at[0, me], load_sem.at[0])
     own.start()
     forwards.append(remote(slots.at[me], arrived.at[1, me], core_send.at[0], core_recv.at[0], other_core()))
     forwards[0].start()
@@ -242,22 +284,30 @@
             remote(arrived.at[0, m], arrived.at[1, m], core_send.at[k], core_recv.at[k], other_core())
         )
         forwards[-1].start()
-    own.wait()
     for d in FAR_FIRST:
+        asks[d].wait_send()
+        answers[d].wait_send()
         copies[d].wait_send()
-    for f in forwards:
-        f.wait()
-
-
-def add_kernel(starts, arrived, block, total):
+    for copy in [own, pass_on] + forwards:
+        copy.wait()
+
+
+def add_kernel(starts, arrived_hbm, block, total, arrived, mine, sems):
+    at = pl.ds(pl.multiple_of(lax.axis_index("grp") * SHARE, SHARE), SHARE)
+    rows = pltpu.make_async_copy(block.at[at], mine, sems.at[2])
+    rows.start()
+    sides = [pltpu.make_async_copy(arrived_hbm.at[i], arrived.at[i], sems.at[i]) for i in range(2)]
+    for copy in sides:
+        copy.start()
     total[...] = jnp.zeros_like(total)
-    at = pl.ds(pl.multiple_of(lax.axis_index("grp") * SHARE, SHARE), SHARE)
-    mine = block[at, :]
+    rows.wait()
+    v = mine[...]
     lane = lax.broadcasted_iota(jnp.int32, (SHARE, 128), 1)
-    left = jnp.where(lane == 0, mine, pltpu.roll(mine, 1, 1))
-    right = jnp.where(lane == 127, mine, pltpu.roll(mine, 127, 1))
-    total[at, :] = BETA * (2.0 * mine - left - right)
+    left = jnp.where(lane == 0, v, pltpu.roll(v, 1, 1))
+    right = jnp.where(lane == 127, v, pltpu.roll(v, 127, 1))
+    total[at, :] = BETA * (2.0 * v - left - right)
     for side in range(2):
+        sides[side].wait()
         for m in range(OWN):
             for k in range(CAP):
                 at = pl.ds(starts[side, m, k], TILE)
@@ -316,59 +366,63 @@
     block = model.reshape(ROWS, 128)
     f32, i32 = jnp.float32, jnp.int32
     dma = pltpu.SemaphoreType.DMA
-    place, request = pl.pallas_call(
+    place, holds, request = pl.pallas_call(
         tables_kernel,
-        out_shape=(jax.ShapeDtypeStruct((TILES,), i32), jax.ShapeDtypeStruct((OWN, 128), i32)),
+        out_shape=(
+            jax.ShapeDtypeStruct((TILES,), i32),
+            jax.ShapeDtypeStruct((OWN * CAP,), i32),
+            jax.ShapeDtypeStruct((OWN, 128), i32),
+        ),
         in_specs=[SMEM, SMEM],
-        out_specs=(SMEM, SMEM),
+        out_specs=(SMEM, SMEM, SMEM),
         scratch_shapes=[pltpu.SMEM((OWN,), i32)],
         name="tables",
     )(owner_ids.transpose(0, 2, 1), offsets)
-    values, starts = pl.pallas_call(
-        fetch_kernel,
+    fields = pltpu.VMEM((S_DEV, 3, TILE + 1, 8, 128), f32)
+    plain = pltpu.VMEM((S_DEV, TILE * 8, 128), f32)
+    arrived, starts = pl.pallas_call(
+        front_kernel,
         out_shape=(
-            jax.ShapeDtypeStruct((OWN, SLOT_ROWS, 128), f32),
+            jax.ShapeDtypeStruct((2, OWN, SLOT_ROWS, 128), f32),
             jax.ShapeDtypeStruct((2, OWN, 128), i32),
         ),
-        in_specs=[SMEM, VMEM],
-        out_specs=(VMEM, SMEM),
-        scratch_shapes=[pltpu.VMEM((OWN, SLOT_ROWS, 128), f32)] + [dma((OWN,))] * 4 + [dma((2,))],
-        compiler_params=pltpu.CompilerParams(collective_id=0, has_side_effects=True),
-        name="fetch",
-    )(request, block)
-    fields = pltpu.VMEM((S_DEV, 3, TILE + 1, 8, 128), f32)
-    slots = pl.pallas_call(
-        solve_kernel,
-        out_shape=jax.ShapeDtypeStruct((OWN * SLOT_ROWS, 128), f32),
-        in_specs=[SMEM, SMEM, VMEM, VMEM, VMEM],
-        out_specs=VMEM,
+        in_specs=[SMEM, SMEM, SMEM, SMEM, HBM, HBM, HBM],
+        out_specs=(HBM, SMEM),
         scratch_shapes=[
-            pltpu.VMEM((S_DEV, TILE * 8, 128), f32),
+            pltpu.VMEM((ROWS, 128), f32),
+            pltpu.VMEM((S_DEV, 3, LZ, TILE * 128), f32),
+            pltpu.VMEM((S_DEV, 3, LZ, TILE * 128), f32),
+            pltpu.VMEM((OWN * SLOT_ROWS, 128), f32),
+            pltpu.VMEM((OWN, SLOT_ROWS, 128), f32),
+            pltpu.VMEM((OWN, SLOT_ROWS, 128), f32),
+            pltpu.VMEM(((TILES + 1) * TILE, 128), f32),
+            plain,
             pltpu.VMEM((S_DEV, TILE, 8, 128), f32),
             fields,
             fields,
             fields,
             pltpu.VMEM((S_DEV, 3, TILE, 8, 128), f32),
-            pltpu.VMEM((S_DEV, TILE * 8, 128), f32),
-        ],
-        compiler_params=pltpu.CompilerParams(vmem_limit_bytes=32 << 20),
-        name="solve",
-    )(place, lengths, values.reshape(OWN * SLOT_ROWS, 128), source, observed)
-    arrived = pl.pallas_call(
-        send_kernel,
-        out_shape=jax.ShapeDtypeStruct((2, OWN, SLOT_ROWS, 128), f32),
-        in_specs=[VMEM],
-        out_specs=VMEM,
-        scratch_shapes=[dma((OWN,))] * 4 + [dma],
-        compiler_params=pltpu.CompilerParams(collective_id=1, has_side_effects=True),
-        name="send",
-    )(slots.reshape(OWN, SLOT_ROWS, 128))
+            plain,
+            dma((3,)),
+        ]
+        + [dma((OWN,))] * 8
+        + [dma((2,))],
+        compiler_params=pltpu.CompilerParams(
+            collective_id=0, has_side_effects=True, vmem_limit_bytes=60 << 20
+        ),
+        name="front",
+    )(place, holds, request, lengths, block, source, observed)
     total = pl.pallas_call(
         add_kernel,
         out_shape=jax.ShapeDtypeStruct((ROWS, 128), f32),
-        in_specs=[SMEM, VMEM, VMEM],
+        in_specs=[SMEM, HBM, HBM],
         out_specs=VMEM,
-        compiler_params=pltpu.CompilerParams(vmem_limit_bytes=32 << 20),
+        scratch_shapes=[
+            pltpu.VMEM((2, OWN, SLOT_ROWS, 128), f32),
+            pltpu.VMEM((SHARE, 128), f32),
+            dma((3,)),
+        ],
+        compiler_params=pltpu.CompilerParams(vmem_limit_bytes=58 << 20),
         name="add",
     )(starts, arrived, block)
     gradient = pl.pallas_call(

time: 84.3 us -> 76.3 us (0.905)
  Pallas kernels: 79 us -> 73.8 us
  local copies, waits for them, and re-layouts: 4.85 us -> 2.2 us
    pallas_call x3 -> x1, Pallas kernels: 49 us -> 41.1 us  [per_device(): pl.pallas_call(front_kernel, out_shape=(jax.ShapeDtypeStruct((2, OWN, SLO...]
    unnamed x19 -> x3, local copies, waits for them, and re-layouts: 4.85 us -> 2.2 us
    pallas_call x1, Pallas kernels: 1.14 us -> 3.51 us  [per_device(): pl.pallas_call(add_kernel, out_shape=jax.ShapeDtypeStruct((ROWS, 128), f3...]
where the time goes in v5:
time: 76.3 us; the launch traced here: 76 us
  Pallas kernels  73.8 us (97%)
  local copies, waits for them, and re-layouts  2.2 us (3%)
    pallas_call x1, Pallas kernels, per_device(): pl.pallas_call(front_kernel, out_shape=(jax.ShapeDtypeStruct((2, OWN, SLO...  41.1 us
    pallas_call x1, Pallas kernels, per_device(): pl.pallas_call(reduce_kernel, out_shape=jax.ShapeDtypeStruct((SHARE, 128)...  27.7 us
    pallas_call x1, Pallas kernels, per_device(): pl.pallas_call(add_kernel, out_shape=jax.ShapeDtypeStruct((ROWS, 128), f3...  3.51 us
    unnamed x3, local copies, waits for them, and re-layouts  2.2 us

profile of v5, /device:TPU:1, one launch (start us, length us, event | category | flops | bytes accessed | tf_op | source)
XLA Modules:
  0.0 76.0 jit_solution(10557710452213757918)
XLA Ops:
  0.0 1.4 %tables.1 = (s32[16]{0:T(128)}, s32[32]{0:T(128)}, s32[8,128]{1,0:T(8,128)}) custom-call(s32[2,1,8]{2,1,0:T(1,128)} %bitcast.12, s32[2,8]{1,0:T(2,128)} %offset.1), custom_call_target="tpu_custom_call" | custom-call | tf_op jit(solution)/shard_map/tables/pallas_call | solution.py:369
  1.4 41.1 %front.1 = (f32[2,8,128,128]{3,2,1,0:T(8,128)}, s32[2,8,128]{2,1,0:T(8,128)}) custom-call(s32[16]{0:T(128)} %get-tuple-element.10.place, s32[32]{0:T(128)} %get-tuple-element.11.holds, s32[8,128]{1,0:T(8,128)} %get-tuple-element.12.request, s32[2,8]{1,0:T(2,128)} %lengths.1, f32[4096,128]{1,0:T(8,128)} %bitcast.10, f32[2,3,8,4096]{3,2,1,0:T(8,128)} %source_hbm.1, ...), custom_call_target="tpu_custom_call" | custom-call | tf_op jit(solution)/shard_map/front/pallas_call | solution.py:383
  42.6 3.5 %add.1 = f32[4096,128]{1,0:T(8,128)} custom-call(s32[2,8,128]{2,1,0:T(8,128)} %get-tuple-element.13.starts, f32[2,8,128,128]{3,2,1,0:T(8,128)} %get-tuple-element.14.arrived_hbm, f32[4096,128]{1,0:T(8,128)} %bitcast.11), custom_call_target="tpu_custom_call" | custom-call | tf_op jit(solution)/shard_map/add/pallas_call | solution.py:415
  46.1 0.0 copy-start
  46.1 1.6 %copy-done = f32[4096,128]{1,0:T(8,128)S(1)} copy-done((f32[4096,128]{1,0:T(8,128)S(1)}, f32[4096,128]{1,0:T(8,128)}, u32[]{:S(2)}) %copy-start) | copy-done | bytes 2097176
  47.7 27.7 %reduce.1 = f32[64,128]{1,0:T(8,128)S(1)} custom-call(f32[8,4,2,64,128]{4,3,2,1,0:T(8,128)S(1)} %bitcast.8), custom_call_target="tpu_custom_call" | custom-call | tf_op jit(solution)/shard_map/reduce/pallas_call | solution.py:428
  75.4 0.6 copy.10
Async XLA Ops:
  46.1 1.6 %copy-start = (f32[4096,128]{1,0:T(8,128)S(1)}, f32[4096,128]{1,0:T(8,128)}, u32[]{:S(2)}) copy-start(f32[4096,128]{1,0:T(8,128)} %add.1) | copy-start | bytes 6291460

commit v6 on v5

--- a/solution.py
+++ b/solution.py
@@ -203,6 +203,7 @@
     observed_hbm,
     arrived,
     starts,
+    smooth,
     block,
     source,
     observed,
@@ -252,6 +253,11 @@
     for k in range(CAP):
         at = pl.ds(me * SLOT_ROWS + k * TILE, TILE)
         values[at, :] = block[pl.ds(starts[0, me, k], TILE), :]
+    mine = block[pl.ds(lax.axis_index("grp") * SHARE, SHARE), :]
+    lane = lax.broadcasted_iota(jnp.int32, (SHARE, 128), 1)
+    left = jnp.where(lane == 0, mine, pltpu.roll(mine, 1, 1))
+    right = jnp.where(lane == 127, mine, pltpu.roll(mine, 127, 1))
+    smooth[...] = BETA * (2.0 * mine - left - right)
     for copy in loads[1:]:
         copy.wait()
     for d in FAR_FIRST:
@@ -292,22 +298,11 @@
         copy.wait()
 
 
-def add_kernel(starts, arrived_hbm, block, total, arrived, mine, sems):
+def add_kernel(starts, arrived, smooth, total):
+    total[...] = jnp.zeros_like(total)
     at = pl.ds(pl.multiple_of(lax.axis_index("grp") * SHARE, SHARE), SHARE)
-    rows = pltpu.make_async_copy(block.at[at], mine, sems.at[2])
-    rows.start()
-    sides = [pltpu.make_async_copy(arrived_hbm.at[i], arrived.at[i], sems.at[i]) for i in range(2)]
-    for copy in sides:
-        copy.start()
-    total[...] = jnp.zeros_like(total)
-    rows.wait()
-    v = mine[...]
-    lane = lax.broadcasted_iota(jnp.int32, (SHARE, 128), 1)
-    left = jnp.where(lane == 0, v, pltpu.roll(v, 1, 1))
-    right = jnp.where(lane == 127, v, pltpu.roll(v, 127, 1))
-    total[at, :] = BETA * (2.0 * v - left - right)
+    total[at, :] = smooth[...]
     for side in range(2):
-        sides[side].wait()
         for m in range(OWN):
             for k in range(CAP):
                 at = pl.ds(starts[side, m, k], TILE)
@@ -380,14 +375,15 @@
     )(owner_ids.transpose(0, 2, 1), offsets)
     fields = pltpu.VMEM((S_DEV, 3, TILE + 1, 8, 128), f32)
     plain = pltpu.VMEM((S_DEV, TILE * 8, 128), f32)
-    arrived, starts = pl.pallas_call(
+    arrived, starts, smooth = pl.pallas_call(
         front_kernel,
         out_shape=(
             jax.ShapeDtypeStruct((2, OWN, SLOT_ROWS, 128), f32),
             jax.ShapeDtypeStruct((2, OWN, 128), i32),
+            jax.ShapeDtypeStruct((SHARE, 128), f32),
         ),
         in_specs=[SMEM, SMEM, SMEM, SMEM, HBM, HBM, HBM],
-        out_specs=(HBM, SMEM),
+        out_specs=(HBM, SMEM, VMEM),
         scratch_shapes=[
             pltpu.VMEM((ROWS, 128), f32),
             pltpu.VMEM((S_DEV, 3, LZ, TILE * 128), f32),
@@ -415,16 +411,11 @@
     total = pl.pallas_call(
         add_kernel,
         out_shape=jax.ShapeDtypeStruct((ROWS, 128), f32),
-        in_specs=[SMEM, HBM, HBM],
+        in_specs=[SMEM, VMEM, VMEM],
         out_specs=VMEM,
-        scratch_shapes=[
-            pltpu.VMEM((2, OWN, SLOT_ROWS, 128), f32),
-            pltpu.VMEM((SHARE, 128), f32),
-            dma((3,)),
-        ],
-        compiler_params=pltpu.CompilerParams(vmem_limit_bytes=58 << 20),
+        compiler_params=pltpu.CompilerParams(vmem_limit_bytes=32 << 20),
         name="add",
-    )(starts, arrived, block)
+    )(starts, arrived, smooth)
     gradient = pl.pallas_call(
         reduce_kernel,
         out_shape=jax.ShapeDtypeStruct((SHARE, 128), f32),

time: 76.3 us -> 75.1 us (0.984)
  Pallas kernels: 73.8 us -> 71.4 us
  local copies, waits for them, and re-layouts: 2.2 us -> 3.29 us
    pallas_call x1, Pallas kernels: 3.51 us -> 1.17 us  [per_device(): pl.pallas_call(add_kernel, out_shape=jax.ShapeDtypeStruct((ROWS, 128), f3...]
    unnamed x3 -> x7, local copies, waits for them, and re-layouts: 2.2 us -> 3.29 us
where the time goes in v6:
time: 75.1 us; the launch traced here: 74.8 us
  Pallas kernels  71.4 us (95%)
  local copies, waits for them, and re-layouts  3.29 us (4%)
    pallas_call x1, Pallas kernels, per_device(): pl.pallas_call(front_kernel, out_shape=(jax.ShapeDtypeStruct((2, OWN, SLO...  41.1 us
    pallas_call x1, Pallas kernels, per_device(): pl.pallas_call(reduce_kernel, out_shape=jax.ShapeDtypeStruct((SHARE, 128)...  27.7 us
    unnamed x7, local copies, waits for them, and re-layouts  3.29 us

profile of v6, /device:TPU:1, one launch (start us, length us, event | category | flops | bytes accessed | tf_op | source)
XLA Modules:
  0.0 74.8 jit_solution(2769674004536893747)
XLA Ops:
  0.0 1.4 %tables.1 = (s32[16]{0:T(128)}, s32[32]{0:T(128)}, s32[8,128]{1,0:T(8,128)}) custom-call(s32[2,1,8]{2,1,0:T(1,128)} %bitcast.11, s32[2,8]{1,0:T(2,128)} %offset.1), custom_call_target="tpu_custom_call" | custom-call | tf_op jit(solution)/shard_map/tables/pallas_call | solution.py:364
  1.4 41.1 %front.1 = (f32[2,8,128,128]{3,2,1,0:T(8,128)}, s32[2,8,128]{2,1,0:T(8,128)}, f32[64,128]{1,0:T(8,128)}) custom-call(s32[16]{0:T(128)} %get-tuple-element.11.place, s32[32]{0:T(128)} %get-tuple-element.12.holds, s32[8,128]{1,0:T(8,128)} %get-tuple-element.13.request, s32[2,8]{1,0:T(2,128)} %lengths.1, f32[4096,128]{1,0:T(8,128)} %bitcast.10, ...), custom_call_target="tpu_custom_call" | custom-call | tf_op jit(solution)/shard_map/front/pallas_call | solution.py:378
  42.6 0.0 copy-start
  42.6 1.2 %copy-done = f32[2,8,128,128]{3,2,1,0:T(8,128)S(1)} copy-done((f32[2,8,128,128]{3,2,1,0:T(8,128)S(1)}, f32[2,8,128,128]{3,2,1,0:T(8,128)}, u32[]{:S(2)}) %copy-start) | copy-done | bytes 1048600
  43.8 0.0 copy-start.1
  43.8 0.8 %copy-done.1 = f32[64,128]{1,0:T(8,128)S(1)} copy-done((f32[64,128]{1,0:T(8,128)S(1)}, f32[64,128]{1,0:T(8,128)}, u32[]{:S(2)}) %copy-start.1) | copy-done | bytes 32792
  44.6 0.0 copy-start.2
  44.6 0.7 copy-done.2
  45.3 1.2 %add.1 = f32[4096,128]{1,0:T(8,128)S(1)} custom-call(s32[2,8,128]{2,1,0:T(8,128)S(1)} %copy-done.2, f32[2,8,128,128]{3,2,1,0:T(8,128)S(1)} %copy-done, f32[64,128]{1,0:T(8,128)S(1)} %copy-done.1), custom_call_target="tpu_custom_call" | custom-call | tf_op jit(solution)/shard_map/add/pallas_call | solution.py:411
  46.4 27.7 %reduce.1 = f32[64,128]{1,0:T(8,128)S(1)} custom-call(f32[8,4,2,64,128]{4,3,2,1,0:T(8,128)S(1)} %bitcast.8), custom_call_target="tpu_custom_call" | custom-call | tf_op jit(solution)/shard_map/reduce/pallas_call | solution.py:419
  74.2 0.6 copy.10
Async XLA Ops:
  42.6 1.2 %copy-start = (f32[2,8,128,128]{3,2,1,0:T(8,128)S(1)}, f32[2,8,128,128]{3,2,1,0:T(8,128)}, u32[]{:S(2)}) copy-start(f32[2,8,128,128]{3,2,1,0:T(8,128)} %get-tuple-element.15.arrived) | copy-start | bytes 3145732
  43.8 0.8 %copy-start.1 = (f32[64,128]{1,0:T(8,128)S(1)}, f32[64,128]{1,0:T(8,128)}, u32[]{:S(2)}) copy-start(f32[64,128]{1,0:T(8,128)} %get-tuple-element.16.smooth) | copy-start | bytes 98308
  44.6 0.7 copy-start.2

commit v7 on v6

--- a/solution.py
+++ b/solution.py
@@ -193,7 +193,41 @@
     by_layer[pl.ds(TILES * TILE, TILE), :] = jnp.zeros((TILE, 128), jnp.float32)
 
 
-def front_kernel(
+NEAR = [(0, 0)] + [d for d in FAR_FIRST if d[0] == 0]
+FAR = [d for d in FAR_FIRST if d[0] == 1]
+OWN_ROWS = NY * SHARE
+BLOCKS = 2 * NX
+
+
+def targets(starts, arrived, vals, senders):
+    lane = lax.broadcasted_iota(jnp.int32, (8, 128), 1)
+    found = []
+    for i, (side, m) in enumerate([(side, m) for m in senders for side in range(2)]):
+        v = arrived[side, m]
+        head = v.astype(jnp.bfloat16)
+        at = pl.ds(i * SLOT_ROWS, SLOT_ROWS)
+        vals[at, pl.ds(0, 128)] = head
+        vals[at, pl.ds(128, 128)] = (v - head.astype(jnp.float32)).astype(jnp.bfloat16)
+        s = [starts[side, m, k] for k in range(CAP)]
+        t = jnp.where(lane < 2 * TILE, jnp.where(lane < TILE, s[0], s[1]), jnp.where(lane < 3 * TILE, s[2], s[3]))
+        found.append(t + lane % TILE)
+    return found
+
+
+def placed_rows(found, vals, rows, j):
+    picked = [
+        jnp.where(rows == (t - j * (2 * OWN_ROWS))[None], 1.0, 0.0).astype(jnp.bfloat16).reshape(OWN_ROWS, 128)
+        for t in found
+    ]
+    d = jnp.dot(jnp.concatenate(picked, 1), vals[...], preferred_element_type=jnp.float32)
+    return (d[:, :128] + d[:, 128:]).reshape(NY, SHARE, 128)
+
+
+CUT = SHARE // 2
+Z_ORDER = [4, 3, 5, 2, 6, 1, 7]
+
+
+def whole_kernel(
     place,
     holds,
     request,
@@ -201,8 +235,9 @@
     block_hbm,
     source_hbm,
     observed_hbm,
+    out,
+    starts,
     arrived,
-    starts,
     smooth,
     block,
     source,
@@ -211,15 +246,23 @@
     outbox,
     slots,
     by_layer,
+    vals,
+    dense,
     *rest,
 ):
-    fields, (load_sem, ask_send, ask_recv, row_send, row_recv, send, recv, core_send, core_recv, core_sem) = (
-        rest[:7],
-        rest[7:],
-    )
+    fields, boxes, sems = rest[:7], rest[7:13], rest[13:]
+    z_box, y_box, z_sum, y_sum, zy_box, yz_box = boxes
+    (load_sem, ask_send, ask_recv, row_send, row_recv, send, recv, core_send, core_recv, core_sem) = sems[:10]
+    z_sem, y_sem, zy_sem, yz_sem = sems[10:]
+    z, y, c, h, x = here()
     me = lax.axis_index("mdl")
+
+    def chip(dz, dy):
+        return ((((z + dz) % NZ) * NY + (y + dy) % NY) * 2 + c, me)
+
     barrier = pltpu.get_barrier_semaphore()
     greeted = [partner(*d)[0] for d in FAR_FIRST] + [other_core()]
+    greeted += [chip(d, 0) for d in Z_ORDER] + [chip(0, d) for d in range(1, NY)]
     for i in greeted:
         pl.semaphore_signal(barrier, inc=1, device_id=i, device_id_type=MESH)
     pairs = ((block_hbm, block), (source_hbm, source), (observed_hbm, observed))
@@ -265,96 +308,83 @@
 
     solve(place, lengths, values, source, observed, by_layer, *fields)
 
-    def fill(m):
+    def fill(m, ref):
         for k in range(CAP):
-            slots[m, pl.ds(k * TILE, TILE), :] = by_layer[pl.ds(holds[m * CAP + k], TILE), :]
-
-    copies, forwards = {}, []
+            ref[m, pl.ds(k * TILE, TILE), :] = by_layer[pl.ds(holds[m * CAP + k], TILE), :]
+
+    copies, forwards = {}, {}
     for dh, dx in FAR_FIRST:
         to, m = partner(dh, dx)
         k = dh * NX + dx
-        fill(m)
+        fill(m, slots)
         copies[dh, dx] = remote(slots.at[m], arrived.at[0, me], send.at[k], recv.at[k], to)
         copies[dh, dx].start()
-    fill(me)
-    own = pltpu.make_async_copy(slots.at[me], arrived.at[0, me], load_sem.at[0])
-    own.start()
-    forwards.append(remote(slots.at[me], arrived.at[1, me], core_send.at[0], core_recv.at[0], other_core()))
-    forwards[0].start()
-    for dh, dx in FAR_FIRST[::-1]:
-        _, m = partner(dh, dx)
-        back = (-dh % 2, -dx % NX)
-        copies[back].wait_recv()
-        k = dh * NX + dx
-        forwards.append(
-            remote(arrived.at[0, m], arrived.at[1, m], core_send.at[k], core_recv.at[k], other_core())
-        )
-        forwards[-1].start()
-    for d in FAR_FIRST:
-        asks[d].wait_send()
-        answers[d].wait_send()
-        copies[d].wait_send()
-    for copy in [own, pass_on] + forwards:
-        copy.wait()
-
-
-def add_kernel(starts, arrived, smooth, total):
-    total[...] = jnp.zeros_like(total)
-    at = pl.ds(pl.multiple_of(lax.axis_index("grp") * SHARE, SHARE), SHARE)
-    total[at, :] = smooth[...]
-    for side in range(2):
-        for m in range(OWN):
-            for k in range(CAP):
-                at = pl.ds(starts[side, m, k], TILE)
-                total[at, :] += arrived[side, m, pl.ds(k * TILE, TILE), :]
-
-
-CUT = SHARE // 2
-Z_ORDER = [4, 3, 5, 2, 6, 1, 7]
-
-
-def reduce_kernel(total, out, z_box, y_box, z_sum, y_sum, zy_box, yz_box, z_sem, y_sem, zy_sem, yz_sem):
-    z, y, c, h, x = here()
-    m = lax.axis_index("mdl")
-
-    def chip(dz, dy):
-        return ((((z + dz) % NZ) * NY + (y + dy) % NY) * 2 + c, m)
-
-    def send(src, dst, sem, i, to):
+    fill(me, arrived.at[0])
+    pass_on.wait()
+
+    def take(steps):
+        for dh, dx in steps:
+            _, m = partner(dh, dx)
+            if (dh, dx) != (0, 0):
+                copies[-dh % 2, -dx % NX].wait_recv()
+            k = dh * NX + dx
+            forwards[dh, dx] = remote(
+                arrived.at[0, m], arrived.at[1, m], core_send.at[k], core_recv.at[k], other_core()
+            )
+            forwards[dh, dx].start()
+        for d in steps:
+            forwards[d].wait_recv()
+        return [partner(*d)[1] for d in steps]
+
+    shape = (OWN_ROWS // 8, 8, 128)
+    at = lax.broadcasted_iota(jnp.int32, shape, 0) * 8 + lax.broadcasted_iota(jnp.int32, shape, 1)
+    rows = (at // SHARE) * (2 * SHARE) + at % SHARE + c * SHARE
+    found = targets(starts, arrived, vals, take(NEAR))
+
+    def near(j, carry):
+        dense[j] = placed_rows(found, vals, rows, j)
+        return carry
+
+    lax.fori_loop(0, NZ, near, 0, unroll=4)
+    found_far = targets(starts, arrived, vals, take(FAR))
+
+    def push(src, dst, sem, i, to):
         copy = remote(src, dst, sem.at[0, i], sem.at[1, i], to)
         copy.start()
         return copy
 
-    meet([chip(d, 0) for d in Z_ORDER] + [chip(0, d) for d in range(1, NY)])
     low, high = pl.ds(0, CUT), pl.ds(CUT, SHARE - CUT)
     along_z, along_y, then_y, then_z = {}, {}, {}, {}
-    for i, d in enumerate(Z_ORDER):
-        if i < NY - 1:
-            e = i + 1
-            along_y[e] = send(total.at[:, (y + e) % NY, c, high, :], y_box.at[e - 1], y_sem, e - 1, chip(0, e))
-        along_z[d] = send(total.at[(z + d) % NZ, :, c, low, :], z_box.at[d - 1], z_sem, d - 1, chip(d, 0))
+    for d in Z_ORDER + [0]:
+        j = (z + d) % NZ
+        dense[j] = dense[j] + placed_rows(found_far, vals, rows, j)
+        if d:
+            along_z[d] = push(dense.at[j, :, low, :], z_box.at[d - 1], z_sem, d - 1, chip(d, 0))
+    for d in (2, 1, 3):
+        along_y[d] = push(dense.at[:, (y + d) % NY, high, :], y_box.at[d - 1], y_sem, d - 1, chip(0, d))
     for copy in along_y.values():
         copy.wait_recv()
     for d in Z_ORDER + [0]:
         j = (z + d) % NZ
-        y_sum[d] = total[j, y, c, high, :] + sum(y_box[k, j] for k in range(NY - 1))
+        y_sum[d] = dense[j, y, high, :] + sum(y_box[k, j] for k in range(NY - 1))
         if d:
-            then_z[d] = send(y_sum.at[d], yz_box.at[d - 1], yz_sem, d - 1, chip(d, 0))
+            then_z[d] = push(y_sum.at[d], yz_box.at[d - 1], yz_sem, d - 1, chip(d, 0))
     for copy in along_z.values():
         copy.wait_recv()
     for d in (2, 1, 3, 0):
         j = (y + d) % NY
-        z_sum[d] = total[z, j, c, low, :] + sum(z_box[k, j] for k in range(NZ - 1))
+        z_sum[d] = dense[z, j, low, :] + sum(z_box[k, j] for k in range(NZ - 1))
         if d:
-            then_y[d] = send(z_sum.at[d], zy_box.at[d - 1], zy_sem, d - 1, chip(0, d))
+            then_y[d] = push(z_sum.at[d], zy_box.at[d - 1], zy_sem, d - 1, chip(0, d))
     for copy in then_z.values():
-        copy.wait()
-    out[high, :] = y_sum[0] + sum(yz_box[k] for k in range(NZ - 1))
+        copy.wait_recv()
+    out[high, :] = smooth[high, :] + y_sum[0] + sum(yz_box[k] for k in range(NZ - 1))
     for copy in then_y.values():
-        copy.wait()
-    out[low, :] = z_sum[0] + sum(zy_box[k] for k in range(NY - 1))
-    for copy in list(along_z.values()) + list(along_y.values()):
-        copy.wait_send()
+        copy.wait_recv()
+    out[low, :] = smooth[low, :] + z_sum[0] + sum(zy_box[k] for k in range(NY - 1))
+    for sent in (asks, answers, copies, forwards, along_z, along_y, then_z, then_y):
+        for copy in sent.values():
+            copy.wait_send()
 
 
 def per_device(model, source, observed, owner_ids, offsets, lengths):
@@ -375,16 +405,15 @@
     )(owner_ids.transpose(0, 2, 1), offsets)
     fields = pltpu.VMEM((S_DEV, 3, TILE + 1, 8, 128), f32)
     plain = pltpu.VMEM((S_DEV, TILE * 8, 128), f32)
-    arrived, starts, smooth = pl.pallas_call(
-        front_kernel,
-        out_shape=(
-            jax.ShapeDtypeStruct((2, OWN, SLOT_ROWS, 128), f32),
-            jax.ShapeDtypeStruct((2, OWN, 128), i32),
-            jax.ShapeDtypeStruct((SHARE, 128), f32),
-        ),
+    gradient = pl.pallas_call(
+        whole_kernel,
+        out_shape=jax.ShapeDtypeStruct((SHARE, 128), f32),
         in_specs=[SMEM, SMEM, SMEM, SMEM, HBM, HBM, HBM],
-        out_specs=(HBM, SMEM, VMEM),
+        out_specs=VMEM,
         scratch_shapes=[
+            pltpu.SMEM((2, OWN, 128), i32),
+            pltpu.VMEM((2, OWN, SLOT_ROWS, 128), f32),
+            pltpu.VMEM((SHARE, 128), f32),
             pltpu.VMEM((ROWS, 128), f32),
             pltpu.VMEM((S_DEV, 3, LZ, TILE * 128), f32),
             pltpu.VMEM((S_DEV, 3, LZ, TILE * 128), f32),
@@ -392,6 +421,8 @@
             pltpu.VMEM((OWN, SLOT_ROWS, 128), f32),
             pltpu.VMEM((OWN, SLOT_ROWS, 128), f32),
             pltpu.VMEM(((TILES + 1) * TILE, 128), f32),
+            pltpu.VMEM((BLOCKS * SLOT_ROWS, 256), jnp.bfloat16),
+            pltpu.VMEM((NZ, NY, SHARE, 128), f32),
             plain,
             pltpu.VMEM((S_DEV, TILE, 8, 128), f32),
             fields,
@@ -399,45 +430,21 @@
             fields,
             pltpu.VMEM((S_DEV, 3, TILE, 8, 128), f32),
             plain,
-            dma((3,)),
-        ]
-        + [dma((OWN,))] * 8
-        + [dma((2,))],
-        compiler_params=pltpu.CompilerParams(
-            collective_id=0, has_side_effects=True, vmem_limit_bytes=60 << 20
-        ),
-        name="front",
-    )(place, holds, request, lengths, block, source, observed)
-    total = pl.pallas_call(
-        add_kernel,
-        out_shape=jax.ShapeDtypeStruct((ROWS, 128), f32),
-        in_specs=[SMEM, VMEM, VMEM],
-        out_specs=VMEM,
-        compiler_params=pltpu.CompilerParams(vmem_limit_bytes=32 << 20),
-        name="add",
-    )(starts, arrived, smooth)
-    gradient = pl.pallas_call(
-        reduce_kernel,
-        out_shape=jax.ShapeDtypeStruct((SHARE, 128), f32),
-        in_specs=[VMEM],
-        out_specs=VMEM,
-        scratch_shapes=[
             pltpu.VMEM((NZ - 1, NY, CUT, 128), f32),
             pltpu.VMEM((NY - 1, NZ, SHARE - CUT, 128), f32),
             pltpu.VMEM((NY, CUT, 128), f32),
             pltpu.VMEM((NZ, SHARE - CUT, 128), f32),
             pltpu.VMEM((NY - 1, CUT, 128), f32),
             pltpu.VMEM((NZ - 1, SHARE - CUT, 128), f32),
-            dma((2, NZ - 1)),
-            dma((2, NY - 1)),
-            dma((2, NY - 1)),
-            dma((2, NZ - 1)),
-        ],
+            dma((3,)),
+        ]
+        + [dma((OWN,))] * 8
+        + [dma((2,)), dma((2, NZ - 1)), dma((2, NY - 1)), dma((2, NY - 1)), dma((2, NZ - 1))],
         compiler_params=pltpu.CompilerParams(
-            collective_id=2, has_side_effects=True, vmem_limit_bytes=32 << 20
+            collective_id=0, has_side_effects=True, vmem_limit_bytes=60 << 20
         ),
-        name="reduce",
-    )(total.reshape(NZ, NY, 2, SHARE, 128))
+        name="whole",
+    )(place, holds, request, lengths, block, source, observed)
     return gradient[:, None, :]
 
 

time: 75.1 us -> 69.9 us (0.931)
  Pallas kernels: 71.4 us -> 68.2 us
  local copies, waits for them, and re-layouts: 3.29 us -> 1.38 us
    pallas_call x3 -> x1, Pallas kernels: 70 us -> 66.8 us  [per_device(): pl.pallas_call(whole_kernel, out_shape=jax.ShapeDtypeStruct((SHARE, 128),...]
    unnamed x7 -> x1, local copies, waits for them, and re-layouts: 3.29 us -> 1.38 us
where the time goes in v7:
time: 69.9 us; the launch traced here: 69.6 us
  Pallas kernels  68.2 us (98%)
  local copies, waits for them, and re-layouts  1.38 us (2%)
    pallas_call x1, Pallas kernels, per_device(): pl.pallas_call(whole_kernel, out_shape=jax.ShapeDtypeStruct((SHARE, 128),...  66.8 us
    pallas_call x1, Pallas kernels, per_device(): pl.pallas_call(tables_kernel, out_shape=(jax.ShapeDtypeStruct((TILES,), i...  1.43 us

profile of v7, /device:TPU:1, one launch (start us, length us, event | category | flops | bytes accessed | tf_op | source)
XLA Modules:
  0.0 69.6 jit_solution(10034667710737276143)
XLA Ops:
  0.0 1.4 %tables.1 = (s32[16]{0:T(128)}, s32[32]{0:T(128)}, s32[8,128]{1,0:T(8,128)}) custom-call(s32[2,1,8]{2,1,0:T(1,128)} %bitcast.9, s32[2,8]{1,0:T(2,128)} %offset.1), custom_call_target="tpu_custom_call" | custom-call | tf_op jit(solution)/shard_map/tables/pallas_call | solution.py:394
  1.4 66.8 %whole.1 = f32[64,128]{1,0:T(8,128)} custom-call(s32[16]{0:T(128)} %get-tuple-element.8.place, s32[32]{0:T(128)} %get-tuple-element.9.holds, s32[8,128]{1,0:T(8,128)} %get-tuple-element.10.request, s32[2,8]{1,0:T(2,128)} %lengths.1, f32[4096,128]{1,0:T(8,128)} %bitcast.7, f32[2,3,8,4096]{3,2,1,0:T(8,128)} %source_hbm.1, f32[2,3,8,4096]{3,2,1,0:T(8,128)} %observed_hbm.1), custom_call_target="tpu_custom_call" | custom-call | tf_op jit(solution)/shard_map/whole/pallas_call | solution.py:408
  68.3 1.4 %copy.10 = f32[64,1,128]{2,1,0:T(1,128)} copy(f32[64,1,128]{2,1,0:T(1,128)} %bitcast.8) | data formatting | bytes 65536

commit v8 on v7

--- a/solution.py
+++ b/solution.py
@@ -58,131 +58,101 @@
     )
 
 
-def tables_kernel(owner, offset, place, holds, request, counts):
-    for o in range(OWN):
-        counts[o] = 0
-        for k in range(CAP):
-            request[o, k] = 0
-            holds[o * CAP + k] = TILES * TILE
-    for t in range(TILES):
-        o = owner[t // LZ, 0, t % LZ]
-        k = counts[o]
-        counts[o] = k + 1
-        place[t] = (o * CAP + k) * TILE
-        holds[o * CAP + k] = t * TILE
-        request[o, k] = offset[t // LZ, t % LZ]
-
-
-BATCH = 4
-
-
-def solve(place, lengths, values, source, observed, by_layer, cond, weight, first, second, third, rhs, part):
+HALF = TILE // 2
+
+
+def half(v):
+    return pltpu.roll(v, 64, 1)
+
+
+def split(a, b):
+    low = lax.broadcasted_iota(jnp.int32, (8, 128), 1) < 64
+    return jnp.where(low, a, half(b)), jnp.where(low, half(a), b)
+
+
+def arrange(source, observed, given):
+    def one(k, carry):
+        places = [pl.ds(pl.multiple_of((k + d) * 128, 128), 128) for d in (0, HALF)]
+        for s in range(S_DEV):
+            for a in range(3):
+                p, q = split(*[source[s, a, :, at] for at in places])
+                given[0, s, a, 2 * k] = -p
+                given[0, s, a, 2 * k + 1] = -q
+                p, q = split(*[observed[s, a, :, at] for at in places])
+                given[1, s, a, 2 * k] = p
+                given[1, s, a, 2 * k + 1] = q
+        return carry
+
+    lax.fori_loop(0, HALF, one, 0, unroll=4)
+
+
+def solve(place, lengths, values, given, by_layer, cond, weight, keeps, state, rhs, part):
     lane = lax.broadcasted_iota(jnp.int32, (8, 128), 1)
     layer = lax.broadcasted_iota(jnp.int32, (8, 128), 0)
+    row = lax.broadcasted_iota(jnp.int32, (TILE, 128), 0)
     low = lane < 64
-    y_next, y_prev = lane % 64 != 63, lane % 64 != 0
-    z_next, z_prev = layer != LZ - 1, layer != 0
-    row = lax.broadcasted_iota(jnp.int32, (TILE, 128), 0)
-
-    def half(v):
-        return pltpu.roll(v, 64, 1)
 
     def shift(mask, by, axis):
-        def one(v):
-            return jnp.where(mask, pltpu.roll(v, by, axis), 0.0)
-
-        return lambda v: one(v) if v.ndim == 2 else jnp.stack([one(v[i]) for i in range(v.shape[0])])
-
-    y_up, y_down = shift(y_next, 127, 1), shift(y_prev, 1, 1)
-    z_up, z_down = shift(z_next, LZ - 1, 0), shift(z_prev, 1, 0)
+        def all_of(v):
+            return jnp.stack([jnp.where(mask, pltpu.roll(v[i], by, axis), 0.0) for i in range(v.shape[0])])
+
+        return all_of
+
+    y_up, y_down = shift(lane % 64 != 63, 127, 1), shift(lane % 64 != 0, 1, 1)
+    z_up, z_down = shift(layer != LZ - 1, LZ - 1, 0), shift(layer != 0, 1, 0)
 
     for t in range(TILES):
         s, z = t // LZ, t % LZ
         got = values[pl.ds(place[t], TILE), :]
         cond[s, pl.ds(z, TILE, stride=8), :] = jnp.where(row < lengths[s, z], jnp.exp(got), AIR)
 
-    def split(a, b):
-        return jnp.where(low, a, half(b)), jnp.where(low, half(a), b)
-
-    def tile(k):
-        return pl.ds(k * 128, 128)
-
-    for k in range(TILE // 2):
+    for k in range(HALF):
         for s in range(S_DEV):
-            pair = split(*[cond[s, pl.ds((k + d) * 8, 8), :] for d in (0, TILE // 2)])
-            ws = [0.5 / (4.0 + c) for c in pair]
+            pair = split(*[cond[s, pl.ds((k + d) * 8, 8), :] for d in (0, HALF)])
             for i in range(2):
-                weight[s, 2 * k + i] = ws[i]
-            for a in range(3):
-                pair = split(source[s, a, :, tile(k)], source[s, a, :, tile(k + TILE // 2)])
-                for i in range(2):
-                    b = ws[i] * pair[i]
-                    rhs[s, a, 2 * k + i] = b
-                    first[s, a, 2 * k + i] = b
-
-    def curl(e, e_x):
-        ex, ey, ez = e
-        hx = (y_up(ez) - ez) - (z_up(ey) - ey)
-        hy = (z_up(ex) - ex) - (e_x[2] - ez)
-        hz = (e_x[1] - ey) - (y_up(ex) - ex)
-        return hx, hy, hz
-
-    def sweep(src, dst):
-        before = []
-        for s in range(S_DEV):
-            ends = [jnp.where(low, half(src[s, a, 0]), 0.0) for a in range(3)]
-            for a in range(1, 3):
-                src[s, a, TILE] = ends[a]
-            _, hy, hz = curl([src[s, a, TILE - 1] for a in range(3)], ends)
-            before.append(tuple(jnp.where(low, 0.0, half(v))[None] for v in (hy, hz)))
-
-        def body(b, carry):
-            at = pl.ds(b * BATCH, BATCH)
-            lasts = []
+                w = 0.5 / (4.0 + pair[i])
+                weight[s, 2 * k + i] = w
+                keeps[s, 2 * k + i] = 0.5 + 4.0 * w
+
+    state[0] = jnp.zeros_like(state[0])
+
+    def phase(p, carry):
+        for r in range(TILE):
             for s in range(S_DEV):
-                e = [src[s, a, at] for a in range(3)]
-                after = pl.ds(b * BATCH + BATCH, 1)
-                e_x = [None] + [jnp.concatenate([e[a][1:], src[s, a, after]], 0) for a in (1, 2)]
-                hx, hy, hz = curl(e, e_x)
-                hy_x = jnp.concatenate([carry[s][0], hy[:-1]], 0)
-                hz_x = jnp.concatenate([carry[s][1], hz[:-1]], 0)
+                for a in range(3):
+                    b = weight[s, r] * (state[p, s, a, r] - given[p, s, a, r])
+                    rhs[s, a, r] = b
+                    state[p + 1, s, a, r] = b
+
+        def sweep(i, carry):
+            for s in range(S_DEV):
+                ex, ey, ez = e = [state[p + 1, s, a] for a in range(3)]
+                ey_x, ez_x = (jnp.concatenate([v[1:], jnp.where(low, half(v[0]), 0.0)[None]], 0) for v in (ey, ez))
+                hx = (y_up(ez) - ez) - (z_up(ey) - ey)
+                hy = (z_up(ex) - ex) - (ez_x - ez)
+                hz = (ey_x - ey) - (y_up(ex) - ex)
+                hy_x, hz_x = (
+                    jnp.concatenate([jnp.where(low, 0.0, half(v[TILE - 1]))[None], v[:-1]], 0) for v in (hy, hz)
+                )
                 back = (
                     (z_down(hy) - hy) - (y_down(hz) - hz),
                     (hz_x - hz) - (z_down(hx) - hx),
                     (y_down(hx) - hx) - (hy_x - hy),
                 )
-                w = weight[s, at]
-                keep = 0.5 + 4.0 * w
+                w, keep = weight[s], keeps[s]
                 for a in range(3):
-                    dst[s, a, at] = keep * e[a] + (rhs[s, a, at] - w * back[a])
-                lasts.append((hy[-1:], hz[-1:]))
-            return tuple(lasts)
-
-        lax.fori_loop(0, TILE // BATCH, body, tuple(before), unroll=4)
-
-    sweep(first, second)
-    sweep(second, first)
-    sweep(first, second)
-
-    for k in range(TILE // 2):
+                    state[p + 1, s, a] = keep * e[a] + (rhs[s, a] - w * back[a])
+            return carry
+
+        lax.fori_loop(0, 3, sweep, 0)
+        return carry
+
+    lax.fori_loop(0, 2, phase, 0)
+
+    for k in range(HALF):
         for s in range(S_DEV):
-            for a in range(3):
-                pair = split(observed[s, a, :, tile(k)], observed[s, a, :, tile(k + TILE // 2)])
-                for i in range(2):
-                    b = weight[s, 2 * k + i] * (second[s, a, 2 * k + i] - pair[i])
-                    rhs[s, a, 2 * k + i] = b
-                    first[s, a, 2 * k + i] = b
-
-    sweep(first, third)
-    sweep(third, first)
-    sweep(first, third)
-
-    for k in range(TILE // 2):
-        for s in range(S_DEV):
-            p, q = (
-                sum(second[s, a, 2 * k + i] * third[s, a, 2 * k + i] for a in range(3)) for i in range(2)
-            )
-            for d, v in ((0, jnp.where(low, p, half(q))), (TILE // 2, jnp.where(low, half(p), q))):
+            pair = [sum(state[1, s, a, 2 * k + i] * state[2, s, a, 2 * k + i] for a in range(3)) for i in range(2)]
+            for d, v in zip((0, HALF), split(*pair)):
                 at = pl.ds((k + d) * 8, 8)
                 part[s, at, :] = -cond[s, at, :] * v
 
@@ -228,17 +198,20 @@
 
 
 def whole_kernel(
-    place,
-    holds,
-    request,
+    owner,
+    offset,
     lengths,
     block_hbm,
     source_hbm,
     observed_hbm,
     out,
+    place,
+    holds,
+    request,
     starts,
     arrived,
     smooth,
+    given,
     block,
     source,
     observed,
@@ -250,7 +223,7 @@
     dense,
     *rest,
 ):
-    fields, boxes, sems = rest[:7], rest[7:13], rest[13:]
+    fields, boxes, sems = rest[:6], rest[6:12], rest[12:]
     z_box, y_box, z_sum, y_sum, zy_box, yz_box = boxes
     (load_sem, ask_send, ask_recv, row_send, row_recv, send, recv, core_send, core_recv, core_sem) = sems[:10]
     z_sem, y_sem, zy_sem, yz_sem = sems[10:]
@@ -269,6 +242,27 @@
     loads = [pltpu.make_async_copy(a, b, load_sem.at[i]) for i, (a, b) in enumerate(pairs)]
     for copy in loads:
         copy.start()
+
+    owners = [owner[t // LZ, 0, t % LZ] for t in range(TILES)]
+    firsts = [offset[t // LZ, t % LZ] for t in range(TILES)]
+    slot_of = []
+    for t in range(TILES):
+        slot = owners[t] * CAP
+        for i in range(t):
+            slot = jnp.where(owners[i] == owners[t], slot + 1, slot)
+        slot_of.append(slot)
+        place[t] = slot * TILE
+
+    def table(j, carry):
+        first, held = jnp.int32(0), jnp.int32(TILES * TILE)
+        for t in range(TILES):
+            first = jnp.where(slot_of[t] == j, firsts[t], first)
+            held = jnp.where(slot_of[t] == j, t * TILE, held)
+        request[j // CAP, j % CAP] = first
+        holds[j] = held
+        return carry
+
+    lax.fori_loop(0, OWN * CAP, table, 0)
     pl.semaphore_wait(barrier, len(greeted))
 
     asks, answers = {}, {}
@@ -303,10 +297,11 @@
     smooth[...] = BETA * (2.0 * mine - left - right)
     for copy in loads[1:]:
         copy.wait()
+    arrange(source, observed, given)
     for d in FAR_FIRST:
         answers[d].wait_recv()
 
-    solve(place, lengths, values, source, observed, by_layer, *fields)
+    solve(place, lengths, values, given, by_layer, *fields)
 
     def fill(m, ref):
         for k in range(CAP):
@@ -391,29 +386,21 @@
     block = model.reshape(ROWS, 128)
     f32, i32 = jnp.float32, jnp.int32
     dma = pltpu.SemaphoreType.DMA
-    place, holds, request = pl.pallas_call(
-        tables_kernel,
-        out_shape=(
-            jax.ShapeDtypeStruct((TILES,), i32),
-            jax.ShapeDtypeStruct((OWN * CAP,), i32),
-            jax.ShapeDtypeStruct((OWN, 128), i32),
-        ),
-        in_specs=[SMEM, SMEM],
-        out_specs=(SMEM, SMEM, SMEM),
-        scratch_shapes=[pltpu.SMEM((OWN,), i32)],
-        name="tables",
-    )(owner_ids.transpose(0, 2, 1), offsets)
-    fields = pltpu.VMEM((S_DEV, 3, TILE + 1, 8, 128), f32)
+    field = (S_DEV, 3, TILE, 8, 128)
     plain = pltpu.VMEM((S_DEV, TILE * 8, 128), f32)
     gradient = pl.pallas_call(
         whole_kernel,
         out_shape=jax.ShapeDtypeStruct((SHARE, 128), f32),
-        in_specs=[SMEM, SMEM, SMEM, SMEM, HBM, HBM, HBM],
+        in_specs=[SMEM, SMEM, SMEM, HBM, HBM, HBM],
         out_specs=VMEM,
         scratch_shapes=[
+            pltpu.SMEM((TILES,), i32),
+            pltpu.SMEM((OWN * CAP,), i32),
+            pltpu.SMEM((OWN, 128), i32),
             pltpu.SMEM((2, OWN, 128), i32),
             pltpu.VMEM((2, OWN, SLOT_ROWS, 128), f32),
             pltpu.VMEM((SHARE, 128), f32),
+            pltpu.VMEM((2,) + field, f32),
             pltpu.VMEM((ROWS, 128), f32),
             pltpu.VMEM((S_DEV, 3, LZ, TILE * 128), f32),
             pltpu.VMEM((S_DEV, 3, LZ, TILE * 128), f32),
@@ -425,10 +412,9 @@
             pltpu.VMEM((NZ, NY, SHARE, 128), f32),
             plain,
             pltpu.VMEM((S_DEV, TILE, 8, 128), f32),
-            fields,
-            fields,
-            fields,
-            pltpu.VMEM((S_DEV, 3, TILE, 8, 128), f32),
+            pltpu.VMEM((S_DEV, TILE, 8, 128), f32),
+            pltpu.VMEM((3,) + field, f32),
+            pltpu.VMEM(field, f32),
             plain,
             pltpu.VMEM((NZ - 1, NY, CUT, 128), f32),
             pltpu.VMEM((NY - 1, NZ, SHARE - CUT, 128), f32),
@@ -444,7 +430,7 @@
             collective_id=0, has_side_effects=True, vmem_limit_bytes=60 << 20
         ),
         name="whole",
-    )(place, holds, request, lengths, block, source, observed)
+    )(owner_ids.transpose(0, 2, 1), offsets, lengths, block, source, observed)
     return gradient[:, None, :]
 
 

time: 69.9 us -> 69.8 us (level)
    pallas_call x1, Pallas kernels: 66.8 us -> 68.3 us  [per_device(): pl.pallas_call(whole_kernel, out_shape=jax.ShapeDtypeStruct((SHARE, 128),...]
    pallas_call x1 -> x0, Pallas kernels: 1.43 us -> none  [per_device(): pl.pallas_call(tables_kernel, out_shape=(jax.ShapeDtypeStruct((TILES,), i...]
where the time goes in v8:
time: 69.8 us; the launch traced here: 69.6 us
  Pallas kernels  68.3 us (98%)
  local copies, waits for them, and re-layouts  1.38 us (2%)
    pallas_call x1, Pallas kernels, per_device(): pl.pallas_call(whole_kernel, out_shape=jax.ShapeDtypeStruct((SHARE, 128),...  68.3 us

profile of v8, /device:TPU:1, one launch (start us, length us, event | category | flops | bytes accessed | tf_op | source)
XLA Modules:
  0.0 69.6 jit_solution(11170895604858332812)
XLA Ops:
  0.0 68.3 %whole.1 = f32[64,128]{1,0:T(8,128)} custom-call(s32[2,1,8]{2,1,0:T(1,128)} %bitcast.9, s32[2,8]{1,0:T(2,128)} %offset.1, s32[2,8]{1,0:T(2,128)} %lengths.1, f32[4096,128]{1,0:T(8,128)} %bitcast.7, f32[2,3,8,4096]{3,2,1,0:T(8,128)} %source_hbm.1, f32[2,3,8,4096]{3,2,1,0:T(8,128)} %observed_hbm.1), custom_call_target="tpu_custom_call" | custom-call | tf_op jit(solution)/shard_map/whole/pallas_call | solution.py:391
  68.3 1.4 %copy.10 = f32[64,1,128]{2,1,0:T(1,128)} copy(f32[64,1,128]{2,1,0:T(1,128)} %bitcast.8) | data formatting | bytes 65536

commit v9 on v8

--- a/solution.py
+++ b/solution.py
@@ -25,7 +25,7 @@
 SMEM = pl.BlockSpec(memory_space=pltpu.SMEM)
 VMEM = pl.BlockSpec(memory_space=pltpu.VMEM)
 HBM = pl.BlockSpec(memory_space=pl.ANY)
-FAR_FIRST = [(1, 2), (1, 1), (1, 3), (1, 0), (0, 2), (0, 1), (0, 3)]
+NEAR_FIRST = [(0, 2), (0, 1), (0, 3), (1, 2), (1, 1), (1, 3), (1, 0)]
 
 
 def here():
@@ -163,8 +163,8 @@
     by_layer[pl.ds(TILES * TILE, TILE), :] = jnp.zeros((TILE, 128), jnp.float32)
 
 
-NEAR = [(0, 0)] + [d for d in FAR_FIRST if d[0] == 0]
-FAR = [d for d in FAR_FIRST if d[0] == 1]
+NEAR = [(0, 0)] + [d for d in NEAR_FIRST if d[0] == 0]
+FAR = [d for d in NEAR_FIRST if d[0] == 1]
 OWN_ROWS = NY * SHARE
 BLOCKS = 2 * NX
 
@@ -234,7 +234,7 @@
         return ((((z + dz) % NZ) * NY + (y + dy) % NY) * 2 + c, me)
 
     barrier = pltpu.get_barrier_semaphore()
-    greeted = [partner(*d)[0] for d in FAR_FIRST] + [other_core()]
+    greeted = [partner(*d)[0] for d in NEAR_FIRST] + [other_core()]
     greeted += [chip(d, 0) for d in Z_ORDER] + [chip(0, d) for d in range(1, NY)]
     for i in greeted:
         pl.semaphore_signal(barrier, inc=1, device_id=i, device_id_type=MESH)
@@ -266,7 +266,7 @@
     pl.semaphore_wait(barrier, len(greeted))
 
     asks, answers = {}, {}
-    for dh, dx in FAR_FIRST:
+    for dh, dx in NEAR_FIRST:
         to, m = partner(dh, dx)
         k = dh * NX + dx
         asks[dh, dx] = remote(request.at[m], starts.at[0, me], ask_send.at[k], ask_recv.at[k], to)
@@ -274,7 +274,7 @@
     for k in range(CAP):
         starts[0, me, k] = request[me, k]
     loads[0].wait()
-    for dh, dx in FAR_FIRST:
+    for dh, dx in NEAR_FIRST:
         back = (-dh % 2, -dx % NX)
         asks[back].wait_recv()
         to, m = partner(dh, dx)
@@ -298,7 +298,7 @@
     for copy in loads[1:]:
         copy.wait()
     arrange(source, observed, given)
-    for d in FAR_FIRST:
+    for d in NEAR_FIRST:
         answers[d].wait_recv()
 
     solve(place, lengths, values, given, by_layer, *fields)
@@ -308,7 +308,7 @@
             ref[m, pl.ds(k * TILE, TILE), :] = by_layer[pl.ds(holds[m * CAP + k], TILE), :]
 
     copies, forwards = {}, {}
-    for dh, dx in FAR_FIRST:
+    for dh, dx in NEAR_FIRST:
         to, m = partner(dh, dx)
         k = dh * NX + dx
         fill(m, slots)
@@ -353,15 +353,21 @@
     for d in Z_ORDER + [0]:
         j = (z + d) % NZ
         dense[j] = dense[j] + placed_rows(found_far, vals, rows, j)
+        for e in (2, 1, 3):
+            along_y[d, e] = remote(
+                dense.at[j, (y + e) % NY, high, :],
+                y_box.at[d, e - 1],
+                y_sem.at[0, d, e - 1],
+                y_sem.at[1, d, e - 1],
+                chip(0, e),
+            )
+            along_y[d, e].start()
         if d:
             along_z[d] = push(dense.at[j, :, low, :], z_box.at[d - 1], z_sem, d - 1, chip(d, 0))
-    for d in (2, 1, 3):
-        along_y[d] = push(dense.at[:, (y + d) % NY, high, :], y_box.at[d - 1], y_sem, d - 1, chip(0, d))
-    for copy in along_y.values():
-        copy.wait_recv()
     for d in Z_ORDER + [0]:
-        j = (z + d) % NZ
-        y_sum[d] = dense[j, y, high, :] + sum(y_box[k, j] for k in range(NY - 1))
+        for e in (2, 1, 3):
+            along_y[d, e].wait_recv()
+        y_sum[d] = dense[(z + d) % NZ, y, high, :] + sum(y_box[d, k] for k in range(NY - 1))
         if d:
             then_z[d] = push(y_sum.at[d], yz_box.at[d - 1], yz_sem, d - 1, chip(d, 0))
     for copy in along_z.values():
@@ -417,7 +423,7 @@
             pltpu.VMEM(field, f32),
             plain,
             pltpu.VMEM((NZ - 1, NY, CUT, 128), f32),
-            pltpu.VMEM((NY - 1, NZ, SHARE - CUT, 128), f32),
+            pltpu.VMEM((NZ, NY - 1, SHARE - CUT, 128), f32),
             pltpu.VMEM((NY, CUT, 128), f32),
             pltpu.VMEM((NZ, SHARE - CUT, 128), f32),
             pltpu.VMEM((NY - 1, CUT, 128), f32),
@@ -425,7 +431,7 @@
             dma((3,)),
         ]
         + [dma((OWN,))] * 8
-        + [dma((2,)), dma((2, NZ - 1)), dma((2, NY - 1)), dma((2, NY - 1)), dma((2, NZ - 1))],
+        + [dma((2,)), dma((2, NZ - 1)), dma((2, NZ, NY - 1)), dma((2, NY - 1)), dma((2, NZ - 1))],
         compiler_params=pltpu.CompilerParams(
             collective_id=0, has_side_effects=True, vmem_limit_bytes=60 << 20
         ),

time: 69.8 us -> 71.1 us (1.019)
  Pallas kernels: 68.3 us -> 69.5 us
    pallas_call x1, Pallas kernels: 68.3 us -> 69.5 us  [per_device(): pl.pallas_call(whole_kernel, out_shape=jax.ShapeDtypeStruct((SHARE, 128),...]
where the time goes in v9:
time: 71.1 us; the launch traced here: 70.9 us
  Pallas kernels  69.5 us (98%)
  local copies, waits for them, and re-layouts  1.38 us (2%)
    pallas_call x1, Pallas kernels, per_device(): pl.pallas_call(whole_kernel, out_shape=jax.ShapeDtypeStruct((SHARE, 128),...  69.5 us

profile of v9, /device:TPU:1, one launch (start us, length us, event | category | flops | bytes accessed | tf_op | source)
XLA Modules:
  0.0 70.9 jit_solution(2139614456418469139)
XLA Ops:
  0.0 69.5 %whole.1 = f32[64,128]{1,0:T(8,128)} custom-call(s32[2,1,8]{2,1,0:T(1,128)} %bitcast.9, s32[2,8]{1,0:T(2,128)} %offset.1, s32[2,8]{1,0:T(2,128)} %lengths.1, f32[4096,128]{1,0:T(8,128)} %bitcast.7, f32[2,3,8,4096]{3,2,1,0:T(8,128)} %source_hbm.1, f32[2,3,8,4096]{3,2,1,0:T(8,128)} %observed_hbm.1), custom_call_target="tpu_custom_call" | custom-call | tf_op jit(solution)/shard_map/whole/pallas_call | solution.py:397
  69.5 1.4 %copy.10 = f32[64,1,128]{2,1,0:T(1,128)} copy(f32[64,1,128]{2,1,0:T(1,128)} %bitcast.8) | data formatting | bytes 65536

commit v10 on v8

--- a/solution.py
+++ b/solution.py
@@ -25,7 +25,7 @@
 SMEM = pl.BlockSpec(memory_space=pltpu.SMEM)
 VMEM = pl.BlockSpec(memory_space=pltpu.VMEM)
 HBM = pl.BlockSpec(memory_space=pl.ANY)
-FAR_FIRST = [(1, 2), (1, 1), (1, 3), (1, 0), (0, 2), (0, 1), (0, 3)]
+NEAR_FIRST = [(0, 2), (0, 1), (0, 3), (1, 2), (1, 1), (1, 3), (1, 0)]
 
 
 def here():
@@ -163,8 +163,8 @@
     by_layer[pl.ds(TILES * TILE, TILE), :] = jnp.zeros((TILE, 128), jnp.float32)
 
 
-NEAR = [(0, 0)] + [d for d in FAR_FIRST if d[0] == 0]
-FAR = [d for d in FAR_FIRST if d[0] == 1]
+NEAR = [(0, 0)] + [d for d in NEAR_FIRST if d[0] == 0]
+FAR = [d for d in NEAR_FIRST if d[0] == 1]
 OWN_ROWS = NY * SHARE
 BLOCKS = 2 * NX
 
@@ -234,7 +234,7 @@
         return ((((z + dz) % NZ) * NY + (y + dy) % NY) * 2 + c, me)
 
     barrier = pltpu.get_barrier_semaphore()
-    greeted = [partner(*d)[0] for d in FAR_FIRST] + [other_core()]
+    greeted = [partner(*d)[0] for d in NEAR_FIRST] + [other_core()]
     greeted += [chip(d, 0) for d in Z_ORDER] + [chip(0, d) for d in range(1, NY)]
     for i in greeted:
         pl.semaphore_signal(barrier, inc=1, device_id=i, device_id_type=MESH)
@@ -253,20 +253,19 @@
         slot_of.append(slot)
         place[t] = slot * TILE
 
-    def table(j, carry):
-        first, held = jnp.int32(0), jnp.int32(TILES * TILE)
-        for t in range(TILES):
-            first = jnp.where(slot_of[t] == j, firsts[t], first)
-            held = jnp.where(slot_of[t] == j, t * TILE, held)
-        request[j // CAP, j % CAP] = first
-        holds[j] = held
+    def ask(o, carry):
+        for k in range(CAP):
+            first = jnp.int32(0)
+            for t in range(TILES):
+                first = jnp.where(slot_of[t] == o * CAP + k, firsts[t], first)
+            request[o, k] = first
         return carry
 
-    lax.fori_loop(0, OWN * CAP, table, 0)
+    lax.fori_loop(0, OWN, ask, 0)
     pl.semaphore_wait(barrier, len(greeted))
 
     asks, answers = {}, {}
-    for dh, dx in FAR_FIRST:
+    for dh, dx in NEAR_FIRST:
         to, m = partner(dh, dx)
         k = dh * NX + dx
         asks[dh, dx] = remote(request.at[m], starts.at[0, me], ask_send.at[k], ask_recv.at[k], to)
@@ -274,7 +273,7 @@
     for k in range(CAP):
         starts[0, me, k] = request[me, k]
     loads[0].wait()
-    for dh, dx in FAR_FIRST:
+    for dh, dx in NEAR_FIRST:
         back = (-dh % 2, -dx % NX)
         asks[back].wait_recv()
         to, m = partner(dh, dx)
@@ -298,7 +297,17 @@
     for copy in loads[1:]:
         copy.wait()
     arrange(source, observed, given)
-    for d in FAR_FIRST:
+
+    def hold(o, carry):
+        for k in range(CAP):
+            held = jnp.int32(TILES * TILE)
+            for t in range(TILES):
+                held = jnp.where(place[t] == (o * CAP + k) * TILE, t * TILE, held)
+            holds[o * CAP + k] = held
+        return carry
+
+    lax.fori_loop(0, OWN, hold, 0)
+    for d in NEAR_FIRST:
         answers[d].wait_recv()
 
     solve(place, lengths, values, given, by_layer, *fields)
@@ -308,7 +317,7 @@
             ref[m, pl.ds(k * TILE, TILE), :] = by_layer[pl.ds(holds[m * CAP + k], TILE), :]
 
     copies, forwards = {}, {}
-    for dh, dx in FAR_FIRST:
+    for dh, dx in NEAR_FIRST:
         to, m = partner(dh, dx)
         k = dh * NX + dx
         fill(m, slots)

time: 69.8 us -> 69.3 us (level)
  no operation moved by 1% of the time
where the time goes in v10:
time: 69.3 us; the launch traced here: 69.1 us
  Pallas kernels  67.8 us (98%)
  local copies, waits for them, and re-layouts  1.38 us (2%)
    pallas_call x1, Pallas kernels, per_device(): pl.pallas_call(whole_kernel, out_shape=jax.ShapeDtypeStruct((SHARE, 128),...  67.8 us

profile of v10, /device:TPU:1, one launch (start us, length us, event | category | flops | bytes accessed | tf_op | source)
XLA Modules:
  0.0 69.1 jit_solution(9817527997945266758)
XLA Ops:
  0.0 67.8 %whole.1 = f32[64,128]{1,0:T(8,128)} custom-call(s32[2,1,8]{2,1,0:T(1,128)} %bitcast.9, s32[2,8]{1,0:T(2,128)} %offset.1, s32[2,8]{1,0:T(2,128)} %lengths.1, f32[4096,128]{1,0:T(8,128)} %bitcast.7, f32[2,3,8,4096]{3,2,1,0:T(8,128)} %source_hbm.1, f32[2,3,8,4096]{3,2,1,0:T(8,128)} %observed_hbm.1), custom_call_target="tpu_custom_call" | custom-call | tf_op jit(solution)/shard_map/whole/pallas_call | solution.py:400
  67.8 1.4 %copy.10 = f32[64,1,128]{2,1,0:T(1,128)} copy(f32[64,1,128]{2,1,0:T(1,128)} %bitcast.8) | data formatting | bytes 65536

commit v11 on v10

--- a/solution.py
+++ b/solution.py
@@ -345,8 +345,8 @@
     rows = (at // SHARE) * (2 * SHARE) + at % SHARE + c * SHARE
     found = targets(starts, arrived, vals, take(NEAR))
 
-    def near(j, carry):
-        dense[j] = placed_rows(found, vals, rows, j)
+    def near(d, carry):
+        dense[d] = placed_rows(found, vals, rows, (z + d) % NZ)
         return carry
 
     lax.fori_loop(0, NZ, near, 0, unroll=4)
@@ -359,25 +359,32 @@
 
     low, high = pl.ds(0, CUT), pl.ds(CUT, SHARE - CUT)
     along_z, along_y, then_y, then_z = {}, {}, {}, {}
-    for d in Z_ORDER + [0]:
-        j = (z + d) % NZ
-        dense[j] = dense[j] + placed_rows(found_far, vals, rows, j)
-        if d:
-            along_z[d] = push(dense.at[j, :, low, :], z_box.at[d - 1], z_sem, d - 1, chip(d, 0))
-    for d in (2, 1, 3):
-        along_y[d] = push(dense.at[:, (y + d) % NY, high, :], y_box.at[d - 1], y_sem, d - 1, chip(0, d))
-    for copy in along_y.values():
-        copy.wait_recv()
-    for d in Z_ORDER + [0]:
-        j = (z + d) % NZ
-        y_sum[d] = dense[j, y, high, :] + sum(y_box[k, j] for k in range(NY - 1))
-        if d:
-            then_z[d] = push(y_sum.at[d], yz_box.at[d - 1], yz_sem, d - 1, chip(d, 0))
+    parts = (4, 5, 6, 7), (3, 2, 1, 0)
+    for part, steps in enumerate(parts):
+        for d in steps:
+            dense[d] = dense[d] + placed_rows(found_far, vals, rows, (z + d) % NZ)
+            if d:
+                along_z[d] = push(dense.at[d, :, low, :], z_box.at[d - 1], z_sem, d - 1, chip(d, 0))
+        for e in (2, 1, 3):
+            along_y[part, e] = push(
+                dense.at[pl.ds(min(steps), 4), (y + e) % NY, high, :],
+                y_box.at[part, e - 1],
+                y_sem,
+                part * (NY - 1) + e - 1,
+                chip(0, e),
+            )
+    for part, steps in enumerate(parts):
+        for e in (2, 1, 3):
+            along_y[part, e].wait_recv()
+        for d in steps:
+            y_sum[d] = dense[d, y, high, :] + sum(y_box[part, k, d % 4] for k in range(NY - 1))
+            if d:
+                then_z[d] = push(y_sum.at[d], yz_box.at[d - 1], yz_sem, d - 1, chip(d, 0))
     for copy in along_z.values():
         copy.wait_recv()
     for d in (2, 1, 3, 0):
         j = (y + d) % NY
-        z_sum[d] = dense[z, j, low, :] + sum(z_box[k, j] for k in range(NZ - 1))
+        z_sum[d] = dense[0, j, low, :] + sum(z_box[k, j] for k in range(NZ - 1))
         if d:
             then_y[d] = push(z_sum.at[d], zy_box.at[d - 1], zy_sem, d - 1, chip(0, d))
     for copy in then_z.values():
@@ -426,7 +433,7 @@
             pltpu.VMEM(field, f32),
             plain,
             pltpu.VMEM((NZ - 1, NY, CUT, 128), f32),
-            pltpu.VMEM((NY - 1, NZ, SHARE - CUT, 128), f32),
+            pltpu.VMEM((2, NY - 1, NZ // 2, SHARE - CUT, 128), f32),
             pltpu.VMEM((NY, CUT, 128), f32),
             pltpu.VMEM((NZ, SHARE - CUT, 128), f32),
             pltpu.VMEM((NY - 1, CUT, 128), f32),
@@ -434,7 +441,7 @@
             dma((3,)),
         ]
         + [dma((OWN,))] * 8
-        + [dma((2,)), dma((2, NZ - 1)), dma((2, NY - 1)), dma((2, NY - 1)), dma((2, NZ - 1))],
+        + [dma((2,)), dma((2, NZ - 1)), dma((2, 2 * (NY - 1))), dma((2, NY - 1)), dma((2, NZ - 1))],
         compiler_params=pltpu.CompilerParams(
             collective_id=0, has_side_effects=True, vmem_limit_bytes=60 << 20
         ),

time: 69.3 us -> 70.6 us (1.019)
  Pallas kernels: 67.8 us -> 69.1 us
    pallas_call x1, Pallas kernels: 67.8 us -> 69.1 us  [per_device(): pl.pallas_call(whole_kernel, out_shape=jax.ShapeDtypeStruct((SHARE, 128),...]
where the time goes in v11:
time: 70.6 us; the launch traced here: 70.5 us
  Pallas kernels  69.1 us (98%)
  local copies, waits for them, and re-layouts  1.38 us (2%)
    pallas_call x1, Pallas kernels, per_device(): pl.pallas_call(whole_kernel, out_shape=jax.ShapeDtypeStruct((SHARE, 128),...  69.1 us

profile of v11, /device:TPU:1, one launch (start us, length us, event | category | flops | bytes accessed | tf_op | source)
XLA Modules:
  0.0 70.5 jit_solution(825965280931723986)
XLA Ops:
  0.0 69.1 %whole.1 = f32[64,128]{1,0:T(8,128)} custom-call(s32[2,1,8]{2,1,0:T(1,128)} %bitcast.9, s32[2,8]{1,0:T(2,128)} %offset.1, s32[2,8]{1,0:T(2,128)} %lengths.1, f32[4096,128]{1,0:T(8,128)} %bitcast.7, f32[2,3,8,4096]{3,2,1,0:T(8,128)} %source_hbm.1, f32[2,3,8,4096]{3,2,1,0:T(8,128)} %observed_hbm.1), custom_call_target="tpu_custom_call" | custom-call | tf_op jit(solution)/shard_map/whole/pallas_call | solution.py:407
  69.1 1.4 %copy.10 = f32[64,1,128]{2,1,0:T(1,128)} copy(f32[64,1,128]{2,1,0:T(1,128)} %bitcast.8) | data formatting | bytes 65536

commit v12 on v11

--- a/solution.py
+++ b/solution.py
@@ -346,7 +346,7 @@
     found = targets(starts, arrived, vals, take(NEAR))
 
     def near(d, carry):
-        dense[d] = placed_rows(found, vals, rows, (z + d) % NZ)
+        dense[d] = placed_rows(found, vals, rows, (z + d + 2) % NZ)
         return carry
 
     lax.fori_loop(0, NZ, near, 0, unroll=4)
@@ -359,15 +359,16 @@
 
     low, high = pl.ds(0, CUT), pl.ds(CUT, SHARE - CUT)
     along_z, along_y, then_y, then_z = {}, {}, {}, {}
-    parts = (4, 5, 6, 7), (3, 2, 1, 0)
+    parts = (4, 3, 5, 2), (6, 1, 7, 0)
     for part, steps in enumerate(parts):
         for d in steps:
-            dense[d] = dense[d] + placed_rows(found_far, vals, rows, (z + d) % NZ)
+            n = (d - 2) % NZ
+            dense[n] = dense[n] + placed_rows(found_far, vals, rows, (z + d) % NZ)
             if d:
-                along_z[d] = push(dense.at[d, :, low, :], z_box.at[d - 1], z_sem, d - 1, chip(d, 0))
+                along_z[d] = push(dense.at[n, :, low, :], z_box.at[d - 1], z_sem, d - 1, chip(d, 0))
         for e in (2, 1, 3):
             along_y[part, e] = push(
-                dense.at[pl.ds(min(steps), 4), (y + e) % NY, high, :],
+                dense.at[pl.ds(part * 4, 4), (y + e) % NY, high, :],
                 y_box.at[part, e - 1],
                 y_sem,
                 part * (NY - 1) + e - 1,
@@ -377,14 +378,14 @@
         for e in (2, 1, 3):
             along_y[part, e].wait_recv()
         for d in steps:
-            y_sum[d] = dense[d, y, high, :] + sum(y_box[part, k, d % 4] for k in range(NY - 1))
+            y_sum[d] = dense[(d - 2) % NZ, y, high, :] + sum(y_box[part, k, (d - 2) % 4] for k in range(NY - 1))
             if d:
                 then_z[d] = push(y_sum.at[d], yz_box.at[d - 1], yz_sem, d - 1, chip(d, 0))
     for copy in along_z.values():
         copy.wait_recv()
     for d in (2, 1, 3, 0):
         j = (y + d) % NY
-        z_sum[d] = dense[0, j, low, :] + sum(z_box[k, j] for k in range(NZ - 1))
+        z_sum[d] = dense[NZ - 2, j, low, :] + sum(z_box[k, j] for k in range(NZ - 1))
         if d:
             then_y[d] = push(z_sum.at[d], zy_box.at[d - 1], zy_sem, d - 1, chip(0, d))
     for copy in then_z.values():

time: 70.6 us -> 70.2 us (level)
  no operation moved by 1% of the time
where the time goes in v12:
time: 70.2 us; the launch traced here: 70 us
  Pallas kernels  68.6 us (98%)
  local copies, waits for them, and re-layouts  1.38 us (2%)
    pallas_call x1, Pallas kernels, per_device(): pl.pallas_call(whole_kernel, out_shape=jax.ShapeDtypeStruct((SHARE, 128),...  68.6 us

profile of v12, /device:TPU:1, one launch (start us, length us, event | category | flops | bytes accessed | tf_op | source)
XLA Modules:
  0.0 70.0 jit_solution(13548275722616663295)
XLA Ops:
  0.0 68.6 %whole.1 = f32[64,128]{1,0:T(8,128)} custom-call(s32[2,1,8]{2,1,0:T(1,128)} %bitcast.9, s32[2,8]{1,0:T(2,128)} %offset.1, s32[2,8]{1,0:T(2,128)} %lengths.1, f32[4096,128]{1,0:T(8,128)} %bitcast.7, f32[2,3,8,4096]{3,2,1,0:T(8,128)} %source_hbm.1, f32[2,3,8,4096]{3,2,1,0:T(8,128)} %observed_hbm.1), custom_call_target="tpu_custom_call" | custom-call | tf_op jit(solution)/shard_map/whole/pallas_call | solution.py:408
  68.6 1.4 %copy.10 = f32[64,1,128]{2,1,0:T(1,128)} copy(f32[64,1,128]{2,1,0:T(1,128)} %bitcast.8) | data formatting | bytes 65536
